TPU v7x, 256 devices: a whole 4x4x8 slice. The times are simulated.
256 devices in a mesh: dp: 32 (over y, z_lo, core), tensor: 8 (over x, z_hi).
Axes of the slice: x: 4, y: 4, z: 8 (z_hi: 2, z_lo: 4; z = z_hi * 4 + z_lo), core: 2. Of those that a mesh axis runs over, the one named last changes fastest.
Arguments:
- attention_output: bfloat16 [32768, 8192], P('dp', 'tensor'), may hold values from -6 to 6
- output_gradient: bfloat16 [32768, 4096], P(('dp', 'tensor')), may hold values from -24 to 24
- codes: bfloat16 [8192, 4096], P('tensor', 'dp'), may hold values from -4 to 4
- block_scale_values: float32 [64, 32], P('tensor', 'dp'), may hold values from 0.004 to 0.02
- adapter_down_factor: bfloat16 [8192, 64], P('tensor'), may hold values from -0.0625 to 0.0625
- adapter_up_factor: bfloat16 [64, 4096], replicated, may hold values from -0.0625 to 0.0625
Outputs:
- input_gradient: bfloat16 [32768, 8192], P('dp', 'tensor')
- down_factor_gradient: float32 [8192, 64], P('tensor')
- up_factor_gradient: float32 [64, 4096], P(None, 'dp')
All inputs are finite; a program needn't handle non-finite values.
Results may differ from a plain program's by a relative error of at most 0.0049.
Values may be sent and summed in bfloat16 or wider, within the bound.
No kernel may reach another device: no remote copies, remote signals or barrier semaphores. Data moves between devices by JAX's collectives and lax.ppermute only.
A program may use at most 128 MiB of HBM per device.

v0:
```python
import jax
import jax.numpy as jnp
from jax import lax
from jax.sharding import PartitionSpec as P

BLOCK = 128


adapter_scale = 2.0
loss_scale_factor = 64.0


def body(
    attention_output,
    output_gradient,
    codes,
    block_scale_values,
    adapter_down_factor,
    adapter_up_factor,
):
    gradient_complete = lax.all_gather(output_gradient, "tensor", axis=0, tiled=True)
    scale_factor = adapter_scale / loss_scale_factor
    projected_rows = lax.dot_general(
        gradient_complete,
        adapter_up_factor,
        (((1,), (1,)), ((), ())),
        preferred_element_type=jnp.float32,
    ).astype(jnp.bfloat16)
    column_scales = jnp.repeat(block_scale_values, BLOCK, axis=1)
    scaled = lax.all_gather(codes.astype(jnp.float32), "dp", axis=1, tiled=True).astype(
        jnp.bfloat16
    ).astype(jnp.float32) * jnp.repeat(
        lax.all_gather(column_scales, "dp", axis=1, tiled=True), BLOCK, axis=0
    )
    base_gradient_part = lax.dot_general(
        gradient_complete,
        scaled.astype(jnp.bfloat16),
        (((1,), (1,)), ((), ())),
        preferred_element_type=jnp.float32,
    )
    adapter_gradient_part = lax.dot_general(
        projected_rows,
        adapter_down_factor,
        (((1,), (1,)), ((), ())),
        preferred_element_type=jnp.float32,
    )
    input_gradient = (base_gradient_part + adapter_scale * adapter_gradient_part).astype(
        jnp.bfloat16
    )
    partial_result = jnp.dot(
        attention_output, adapter_down_factor, preferred_element_type=jnp.float32
    )
    adapter_output = lax.psum(partial_result, "tensor").astype(jnp.bfloat16)
    adapter_term = scale_factor * jnp.dot(
        adapter_output.T, gradient_complete, preferred_element_type=jnp.float32
    )
    up_factor_gradient = lax.psum_scatter(adapter_term, "dp", scatter_dimension=1, tiled=True)
    down_factor_term = scale_factor * jnp.dot(
        attention_output.T, projected_rows, preferred_element_type=jnp.float32
    )
    down_factor_gradient = lax.psum(down_factor_term, "dp")
    return (input_gradient, down_factor_gradient, up_factor_gradient)


def solution(mesh):
    placed = (
        P("dp", "tensor"),
        P(("dp", "tensor"), None),
        P("tensor", "dp"),
        P("tensor", "dp"),
        P("tensor", None),
        P(),
    )
    return jax.shard_map(
        body,
        mesh=mesh,
        in_specs=placed,
        out_specs=(P("dp", "tensor"), P("tensor", None), P(None, "dp")),
        check_vma=False,
    )
```

profile of v0, /device:TPU:1, one launch (start us, length us, event | category | flops | bytes accessed | tf_op | source)
XLA Modules:
  0.0 729.0 jit_solution(6628580762881066477)
XLA Ops:
  7.2 0.0 all-gather.5.cloned.1.call-start
  7.2 0.7 all-gather.5.cloned.1.call-update
  7.9 0.0 all-gather.3.cloned.1.call-start
  8.0 0.7 all-gather.3.cloned.1.call-update
  8.7 0.0 all-reduce.3.cloned.1.call-start
  8.7 0.1 copy-done
  8.8 1.6 fusion.5
  10.4 0.7 reshape.13
  11.1 53.1 %all_gather.10 = f32[8,4096]{1,0:T(8,128)S(1)} all-gather(f32[8,128]{1,0:T(8,128)S(1)} %reshape.13), channel_id=1, replica_groups=mesh['dp'=32,'tensor'=8] {'dp'}, dimensions={1}, use_global_device_ids=true | all-gather | bytes 135168 | tf_op jit(solution)/shard_map/all_gather | solution.py:33
  64.2 126.6 %all-reduce.4 = bf16[1024,64]{1,0:T(8,128)(2,1)S(1)} all-reduce(f32[1024,64]{1,0:T(8,128)S(1)} %fusion.5), channel_id=1, replica_groups=mesh['dp'=32,'tensor'=8] {'tensor'}, use_global_device_ids=true, to_apply=%region_1.0 | all-reduce | flops 65536 | bytes 393216 | tf_op jit(solution)/shard_map/psum | solution.py:53
  190.8 27.8 %all-gather.5.cloned.1.call-done = bf16[1024,4096]{1,0:T(8,128)(2,1)} async-done(((bf16[128,4096]{1,0:T(8,128)(2,1)}), bf16[1024,4096]{1,0:T(8,128)(2,1)}) %all-gather.5.cloned.1.call-update) | async-done | bytes 8388624 | tf_op jit(solution)/shard_map/all_gather | solution.py:21
  218.7 6.1 convolution_convert_fusion
  224.7 1.2 fusion.2
  225.9 0.0 all-reduce.3.cloned.1.call-update
  226.0 0.0 reduce-scatter.2.cloned.1.call-start
  226.0 6.2 convolution_multiply_fusion
  232.2 71.3 %all-gather.3.cloned.1.call-done = bf16[1024,4096]{1,0:T(8,128)(2,1)} async-done(((bf16[1024,128]{1,0:T(8,128)(2,1)}), bf16[1024,4096]{1,0:T(8,128)(2,1)}) %all-gather.3.cloned.1.call-update) | async-done | bytes 8388624 | tf_op jit(solution)/shard_map/all_gather | solution.py:30
  303.6 9.3 %fusion = bf16[1024,4096]{1,0:T(8,128)(2,1)} fusion(f32[8,4096]{1,0:T(8,128)S(1)} %all_gather.10, bf16[1024,4096]{1,0:T(8,128)(2,1)} %all-gather.3.cloned.1.call-done), kind=kLoop, calls=%fused_computation.1 | loop fusion | flops 12582912 | bytes 16908288 | tf_op jit(solution)/shard_map/convert_element_type | solution.py:37
  312.9 12.7 %fusion.4 = f32[1024,1024]{1,0:T(8,128)S(1)} fusion(bf16[1024,4096]{1,0:T(8,128)(2,1)} %fusion, bf16[1024,4096]{1,0:T(8,128)(2,1)} %all-gather.5.cloned.1.call-done), kind=kOutput, calls=%fused_computation.9 | convolution fusion | flops 8589934592 | bytes 20971520 | tf_op jit(solution)/shard_map/dot_general | solution.py:35
  325.6 2.1 fusion.1
  327.7 3.9 copy.10
  331.6 247.7 %all-reduce.3.cloned.1.call-done = f32[1024,64]{0,1:T(8,128)} async-done(((f32[1024,64]{0,1:T(8,128)}), f32[1024,64]{0,1:T(8,128)}) %all-reduce.3.cloned.1.call-update) | async-done | bytes 262160 | tf_op jit(solution)/shard_map/psum | solution.py:61
  579.3 141.5 %reduce-scatter.2.cloned.1.call-done = f32[64,128]{1,0:T(8,128)} async-done(((f32[64,4096]{1,0:T(8,128)}), f32[64,128]{1,0:T(8,128)}) %reduce-scatter.2.cloned.1.call-update) | async-done | bytes 32784 | tf_op jit(solution)/shard_map/reduce_scatter | solution.py:57
  720.8 1.7 copy.15
  (4 shorter events, 0.0 us)
Async XLA Ops:
  7.2 1.6 copy-start
  7.2 211.5 %all-gather.5.cloned.1.call-start = ((), (), s32[]{:S(2)}) async-start(), calls=%async_computation.2 | async-start | bytes 9437184 | tf_op jit(solution)/shard_map/all_gather | solution.py:21
  7.9 295.7 %all-gather.3.cloned.1.call-start = ((), (), s32[]{:S(2)}) async-start(), calls=%async_computation.1 | async-start | bytes 8650752 | tf_op jit(solution)/shard_map/all_gather | solution.py:30
  8.7 570.6 %all-reduce.3.cloned.1.call-start = ((), (), s32[]{:S(2)}) async-start(), calls=%async_computation.3 | async-start | bytes 524288 | tf_op jit(solution)/shard_map/psum | solution.py:61
  226.0 494.8 %reduce-scatter.2.cloned.1.call-start = ((), (), s32[]{:S(2)}) async-start(), calls=%async_computation.4 | async-start | bytes 1081344 | tf_op jit(solution)/shard_map/reduce_scatter | solution.py:57
  312.9 12.7 %copy-start.1 = (bf16[1024,64]{0,1:T(8,128)(2,1)S(1)}, bf16[1024,64]{0,1:T(8,128)(2,1)}, u32[]{:S(2)}) copy-start(bf16[1024,64]{0,1:T(8,128)(2,1)} %param.10) | copy-start | bytes 393220
Sparse Core Ops, SparseCore 0:
  10.6 207.9 all-gather.4
  220.4 83.1 all-gather.2
  306.8 272.4 all-reduce.2
  582.3 138.4 reduce-scatter.1
where the time goes:
time: 734 us; the launch traced here: 729 us
  waiting for transfers between devices  490 us (67%)
  blocking collectives  180 us (25%)
  matrix products  29.8 us (4%)
  between operations  13.8 us (2%)
  other arithmetic  9.31 us (1%)
    psum x1, waiting for transfers between devices, body(): down_factor_gradient = lax.psum(down_factor_term, 'dp')  248 us
    reduce_scatter x1, waiting for transfers between devices, body(): lax.psum_scatter(adapter_term, 'dp', scatter_dimension=1, tiled=True)  142 us
    psum x1, blocking collectives, body(): adapter_output = lax.psum(partial_result, 'tensor').astype(jnp.bfloat16)  127 us
    all_gather x1, waiting for transfers between devices, body(): lax.all_gather(codes.astype(jnp.float32), 'dp', axis=1, tiled=True)  71.3 us
    all_gather x1, blocking collectives, body(): lax.all_gather(column_scales, 'dp', axis=1, tiled=True)  53.1 us
    all_gather x1, waiting for transfers between devices, body(): lax.all_gather(output_gradient, 'tensor', axis=0, tiled=True)  27.8 us
  transfers between devices with their start and end apart: 4, of which 4 were waited for; matrix products, arithmetic and copies ran while one was open for 6% of the time, Pallas kernels for 0%

commit v1 on v0

v1 whole, which is shorter than its diff:
```python
import functools

import jax
import jax.numpy as jnp
from jax import lax
from jax.experimental import pallas as pl
from jax.experimental.pallas import tpu as pltpu
from jax.sharding import PartitionSpec as P

BLOCK = 128
NX = 4
ROWS = 128
K_CHUNK = 1024
M_TILE = 256

adapter_scale = 2.0
loss_scale_factor = 64.0


def hi_swap(value):
    return lax.ppermute(value, "tensor", [(t, t ^ 1) for t in range(2 * NX)])


def x_shift(value, step):
    return lax.ppermute(
        value,
        "tensor",
        [(t, ((t // 2 + step) % NX) * 2 + t % 2) for t in range(2 * NX)],
    )


def x_gather(own):
    half = own.shape[0] // 2
    before = x_shift(own, 1)
    after = x_shift(own, -1)
    far_top = x_shift(before[:half], 1)
    far_bottom = x_shift(after[half:], -1)
    return [(own, 0, 0), (before, -1, 0), (after, 1, 0), (far_top, 2, 0), (far_bottom, 2, half)]


def product_kernel(places, count, *refs):
    pieces = refs[:count]
    weights, projected, down, out, g_all, w_all, total, g_sem, w_sem = refs[count:]
    tensor = lax.axis_index("tensor")
    x, hi = tensor // 2, tensor % 2
    chunks = w_all.shape[0] // K_CHUNK

    def piece_copies(k):
        columns = pl.ds(k * K_CHUNK, K_CHUNK)
        for p, (ref, (flip, dx, start)) in enumerate(zip(pieces, places)):
            other = lax.rem(x + dx + NX, NX) * 2 + (1 - hi if flip else hi)
            at = pl.multiple_of(other * ROWS + start, 32)
            yield pltpu.make_async_copy(
                ref.at[:, columns], g_all.at[pl.ds(at, ref.shape[0]), columns], g_sem.at[k, p]
            )

    def weight_copy(k):
        rows = pl.ds(k * K_CHUNK, K_CHUNK)
        return pltpu.make_async_copy(weights.at[rows], w_all.at[rows], w_sem.at[k])

    for k in range(chunks):
        weight_copy(k).start()
        for copy in piece_copies(k):
            copy.start()

    tiles = g_all.shape[0] // M_TILE
    for k in range(chunks):
        weight_copy(k).wait()
        for copy in piece_copies(k):
            copy.wait()

        def tile(i, carry, k=k):
            rows = pl.ds(pl.multiple_of(i * M_TILE, M_TILE), M_TILE)
            columns = pl.ds(k * K_CHUNK, K_CHUNK)
            part = jnp.dot(
                g_all[rows, columns], w_all[columns, :], preferred_element_type=jnp.float32
            )
            if k == 0:
                part += adapter_scale * lax.dot_general(
                    projected[rows, :],
                    down[...],
                    (((1,), (1,)), ((), ())),
                    preferred_element_type=jnp.float32,
                )
            else:
                part += total[rows, :]
            if k == chunks - 1:
                out[rows, :] = part.astype(out.dtype)
            else:
                total[rows, :] = part
            return carry

        lax.fori_loop(0, tiles, tile, 0)


def product(pieces, places, weights, projected, down):
    tokens, width = projected.shape[0], weights.shape[1]
    depth = weights.shape[0]
    chunks = depth // K_CHUNK
    whole = pl.BlockSpec(memory_space=pltpu.VMEM)
    outside = pl.BlockSpec(memory_space=pl.ANY)
    return pl.pallas_call(
        functools.partial(product_kernel, places, len(pieces)),
        out_shape=jax.ShapeDtypeStruct((tokens, width), jnp.bfloat16),
        in_specs=[outside] * (len(pieces) + 1) + [whole, whole],
        out_specs=whole,
        scratch_shapes=[
            pltpu.VMEM((tokens, depth), jnp.bfloat16),
            pltpu.VMEM((depth, width), jnp.bfloat16),
            pltpu.VMEM((tokens, width), jnp.float32),
            pltpu.SemaphoreType.DMA((chunks, len(pieces))),
            pltpu.SemaphoreType.DMA((chunks,)),
        ],
        compiler_params=pltpu.CompilerParams(vmem_limit_bytes=40 * 1024 * 1024),
        cost_estimate=pl.CostEstimate(
            flops=2 * tokens * width * depth,
            bytes_accessed=2 * (tokens + width) * depth + 2 * tokens * width,
            transcendentals=0,
        ),
    )(*pieces, weights, projected, down)


def tensor_sum(value):
    value = value + hi_swap(value)
    for partner in ((1, 0, 3, 2), (3, 2, 1, 0)):
        moved = lax.ppermute(
            value, "tensor", [(t, partner[t // 2] * 2 + t % 2) for t in range(2 * NX)]
        )
        value = value + moved
    return value


def body(
    attention_output,
    output_gradient,
    codes,
    block_scale_values,
    adapter_down_factor,
    adapter_up_factor,
):
    f32, bf16 = jnp.float32, jnp.bfloat16
    scale_factor = adapter_scale / loss_scale_factor
    n_dp = lax.axis_size("dp")
    n_tensor = lax.axis_size("tensor")

    scaled = (codes.astype(f32) * jnp.repeat(block_scale_values, BLOCK, axis=0)).astype(bf16)
    weights = lax.all_gather(scaled.T, "dp", axis=0, tiled=True)

    half = ROWS // 2
    other = [hi_swap(output_gradient[:half]), hi_swap(output_gradient[half:])]
    pieces, places = [], []
    for flip, base, own in (
        (0, 0, output_gradient),
        (1, 0, other[0]),
        (1, half, other[1]),
    ):
        for value, dx, start in x_gather(own):
            pieces.append(value)
            places.append((flip, dx, base + start))

    projected_own = lax.dot_general(
        output_gradient, adapter_up_factor, (((1,), (1,)), ((), ())), preferred_element_type=f32
    ).astype(bf16)
    partial_result = jnp.dot(attention_output, adapter_down_factor, preferred_element_type=f32)
    parcel = jnp.concatenate(
        [
            partial_result.reshape(n_tensor, ROWS, -1),
            jnp.broadcast_to(projected_own.astype(f32)[None], (n_tensor,) + projected_own.shape),
        ],
        axis=2,
    )
    parcel = lax.all_to_all(parcel, "tensor", 0, 0, tiled=True)
    rank = adapter_down_factor.shape[1]
    adapted = jnp.sum(parcel[:, :, :rank], axis=0).astype(bf16)
    projected = parcel[:, :, rank:].reshape(n_tensor * ROWS, rank).astype(bf16)

    up_term = lax.dot_general(
        adapted, output_gradient, (((0,), (0,)), ((), ())), preferred_element_type=f32
    )
    down_term = lax.dot_general(
        attention_output, projected, (((0,), (0,)), ((), ())), preferred_element_type=f32
    )
    up_parcel = up_term.reshape(rank, n_dp, -1).transpose(1, 0, 2)
    down_parcel = down_term.reshape(n_dp, -1, up_parcel.shape[2])
    second = lax.all_to_all(
        jnp.concatenate([up_parcel, down_parcel], axis=1), "dp", 0, 0, tiled=True
    )
    summed = scale_factor * jnp.sum(second, axis=0)
    up_factor_gradient = tensor_sum(summed[:rank])
    down_part = summed[rank:]
    down_factor_gradient = lax.all_to_all(
        jnp.broadcast_to(down_part[None], (n_dp,) + down_part.shape), "dp", 0, 0, tiled=True
    ).reshape(-1, rank)

    input_gradient = product(pieces, places, weights, projected, adapter_down_factor)
    return (input_gradient, down_factor_gradient, up_factor_gradient)


def solution(mesh):
    placed = (
        P("dp", "tensor"),
        P(("dp", "tensor"), None),
        P("tensor", "dp"),
        P("tensor", "dp"),
        P("tensor", None),
        P(),
    )
    return jax.shard_map(
        body,
        mesh=mesh,
        in_specs=placed,
        out_specs=(P("dp", "tensor"), P("tensor", None), P(None, "dp")),
        check_vma=False,
    )
```

time: 734 us -> 231 us (0.31)
  waiting for transfers between devices: 490 us -> 91.9 us
  blocking collectives: 180 us -> 32 us
  starting transfers between devices: 0.16 us -> 35.7 us
  matrix products: 29.8 us -> 4.07 us
  local copies, waits for them, and re-layouts: 6.39 us -> 26.9 us
  Pallas kernels: 0 us -> 16.5 us
    psum x1 -> x0, waiting for transfers between devices: 248 us -> none  [body(): down_factor_gradient = lax.psum(down_factor_term, 'dp')]
    reduce_scatter x1 -> x0, waiting for transfers between devices: 142 us -> none  [body(): lax.psum_scatter(adapter_term, 'dp', scatter_dimension=1, tiled=True)]
    psum x1 -> x0, blocking collectives: 127 us -> none  [body(): adapter_output = lax.psum(partial_result, 'tensor').astype(jnp.bfloat16)]
    all_gather x2 -> x1, waiting for transfers between devices: 99.1 us -> 0.01 us  [body(): weights = lax.all_gather(scaled.T, 'dp', axis=0, tiled=True)]
    ppermute x0 -> x17, waiting for transfers between devices: none -> 75.7 us  [the longest x3 70.2 us: hi_swap(): return lax.ppermute(value, 'tensor', [(t, t ^ 1) for t in range(2 * NX)])]
    all_gather x1 -> x0, blocking collectives: 53.1 us -> none  [body(): lax.all_gather(column_scales, 'dp', axis=1, tiled=True)]
    all_to_all x0 -> x1, blocking collectives: none -> 32 us  [body(): parcel = lax.all_to_all(parcel, 'tensor', 0, 0, tiled=True)]
    dot_general x6 -> x3, matrix products: 29.8 us -> 3.38 us  [the longest x1 1.84 us: body(): lax.dot_general(output_gradient, adapter_up_factor, (((1,), (1,)), ((), (...]
  transfers between devices with their start and end apart: 4 -> 20, of which waited for: 4 -> 5; matrix products, arithmetic and copies ran while one was open for 6% -> 14% of each run, Pallas kernels for 0% -> 0%
where the time goes in v1:
time: 231 us; the launch traced here: 230 us
  waiting for transfers between devices  91.9 us (40%)
  starting transfers between devices  35.7 us (15%)
  blocking collectives  32 us (14%)
  local copies, waits for them, and re-layouts  26.9 us (12%)
  Pallas kernels  16.5 us (7%)
  between operations  14.3 us (6%)
  other arithmetic  8.16 us (4%)
  matrix products  4.07 us (2%)
    ppermute x3, waiting for transfers between devices, hi_swap(): return lax.ppermute(value, 'tensor', [(t, t ^ 1) for t in range(2 * NX)])  70.2 us
    all_to_all x1, blocking collectives, body(): parcel = lax.all_to_all(parcel, 'tensor', 0, 0, tiled=True)  32 us
    pallas_call x1, Pallas kernels, product(): pl.pallas_call(functools.partial(product_kernel, places, len(pieces)), ou...  16.5 us
    all_to_all x1, waiting for transfers between devices, body(): lax.all_to_all(jnp.concatenate([up_parcel, down_parcel], axis=1), 'dp', 0...  16.2 us
    all_to_all x1, starting transfers between devices, body(): lax.all_to_all(jnp.concatenate([up_parcel, down_parcel], axis=1), 'dp', 0...  11.2 us
    ppermute x12, starting transfers between devices, x_shift(): lax.ppermute(value, 'tensor', [(t, (t // 2 + step) % NX * 2 + t % 2) for...  10.8 us
    unnamed x23, local copies, waits for them, and re-layouts  7.99 us
    all_to_all x1, starting transfers between devices, body(): lax.all_to_all(jnp.broadcast_to(down_part[None], (n_dp,) + down_part.shap...  5.92 us
  transfers between devices with their start and end apart: 20, of which 5 were waited for; matrix products, arithmetic and copies ran while one was open for 14% of the time, Pallas kernels for 0%

profile of v1, /device:TPU:1, one launch (start us, length us, event | category | flops | bytes accessed | tf_op | source)
XLA Modules:
  0.0 229.6 jit_solution(13209959194314587107)
XLA Ops:
  10.0 1.8 fusion
  12.9 32.0 %all_to_all.15 = f32[8,128,128]{2,1,0:T(8,128)S(1)} all-to-all(f32[8,128,128]{2,1,0:T(8,128)S(1)} %pad_maximum_fusion.1), channel_id=1, replica_groups=mesh['dp'=32,'tensor'=8] {'tensor'}, dimensions={0} | all-to-all | bytes 1048576 | tf_op jit(solution)/shard_map/all_to_all | solution.py:172
  47.0 2.0 copy.25
  48.9 1.9 reshape.29
  54.0 11.2 %all-to-all-start.1 = ((f32[32,80,128]{2,1,0:T(8,128)}), f32[32,80,128]{2,1,0:T(8,128)}, u32[]{:S(2)}, u32[]{:S(2)}) async-start(f32[32,80,128]{2,1,0:T(8,128)} %pad_maximum_fusion), calls=%async_computation.1 | async-start | bytes 2621440 | tf_op jit(solution)/shard_map/all_to_all | solution.py:185
  66.1 2.7 %collective-permute-start.1 = (bf16[128,4096]{1,0:T(8,128)(2,1)S(1)}, bf16[128,4096]{1,0:T(8,128)(2,1)}, u32[]{:S(2)}, u32[]{:S(2)}) collective-permute-start(bf16[128,4096]{1,0:T(8,128)(2,1)S(1)} %copy-done.1), channel_id=1, source_target_pairs={{0,6},{1,7},{2,0},{3,1},{4,2},{5,3},{6,4},{7,5},{8,14},{9,15},{10,... | collective-permute-start | bytes 3145736 | tf_op jit(solution)/shard_map/ppermute | solution.py:25
  68.7 5.4 %collective-permute-start.4 = (bf16[64,4096]{1,0:T(8,128)(2,1)}, bf16[64,4096]{1,0:T(8,128)(2,1)}, u32[]{:S(2)}, u32[]{:S(2)}) collective-permute-start(bf16[64,4096]{1,0:T(8,128)(2,1)} %get-tuple-element.10), channel_id=1, source_target_pairs={{0,1},{1,0},{2,3},{3,2},{4,5},{5,4},{6,7},{7,6},{8,9},{9,8},{10,11... | collective-permute-start | bytes 1572872 | tf_op jit(solution)/shard_map/ppermute | solution.py:21
  74.1 63.7 %collective-permute-done.9.refs_10_ = bf16[64,4096]{1,0:T(8,128)(2,1)} collective-permute-done((bf16[64,4096]{1,0:T(8,128)(2,1)S(1)}, bf16[64,4096]{1,0:T(8,128)(2,1)}, u32[]{:S(2)}, u32[]{:S(2)}) %collective-permute-start.9) | collective-permute-done | bytes 524320 | tf_op jit(solution)/shard_map/ppermute | solution.py:21
  140.5 16.2 %all-to-all-done.1 = f32[32,80,128]{2,1,0:T(8,128)} async-done(((f32[32,80,128]{2,1,0:T(8,128)}), f32[32,80,128]{2,1,0:T(8,128)}, u32[]{:S(2)}, u32[]{:S(2)}) %all-to-all-start.1) | async-done | bytes 1310752 | tf_op jit(solution)/shard_map/all_to_all | solution.py:185
  156.7 2.0 reduce_sum.19
  159.7 6.6 %collective-permute-done.14 = f32[64,128]{1,0:T(8,128)S(1)} collective-permute-done((f32[64,128]{1,0:T(8,128)S(1)}, f32[64,128]{1,0:T(8,128)S(1)}, u32[]{:S(2)}, u32[]{:S(2)}) %collective-permute-start.14) | collective-permute-done | bytes 32800 | tf_op jit(solution)/shard_map/ppermute | solution.py:21
  167.8 1.7 slice.53
  170.3 1.9 slice.49
  172.1 1.9 slice.50
  174.0 4.4 %collective-permute-done.15 = f32[64,128]{1,0:T(8,128)S(1)} collective-permute-done((f32[64,128]{1,0:T(8,128)S(1)}, f32[64,128]{1,0:T(8,128)S(1)}, u32[]{:S(2)}, u32[]{:S(2)}) %collective-permute-start.15) | collective-permute-done | bytes 32800 | tf_op jit(solution)/shard_map/ppermute | solution.py:126
  179.8 5.9 %all-to-all-start.2 = ((f32[32,16,128]{2,1,0:T(8,128)}), f32[32,16,128]{2,1,0:T(8,128)}, u32[]{:S(2)}, u32[]{:S(2)}) async-start(f32[32,16,128]{2,1,0:T(8,128)} %broadcast_in_dim.20), calls=%async_computation.2 | async-start | bytes 524288 | tf_op jit(solution)/shard_map/all_to_all | solution.py:191
  187.1 1.6 collective-permute-start.16
  188.7 1.7 slice.54
  190.4 1.7 slice.51
  193.1 1.7 slice.52
  195.8 2.3 %collective-permute-start.8 = (bf16[32,4096]{1,0:T(8,128)(2,1)}, bf16[32,4096]{1,0:T(8,128)(2,1)}, u32[]{:S(2)}, u32[]{:S(2)}) collective-permute-start(bf16[32,4096]{1,0:T(8,128)(2,1)} %slice.52), channel_id=1, source_target_pairs={{0,6},{1,7},{2,0},{3,1},{4,2},{5,3},{6,4},{7,5},{8,14},{9,15},{10,... | collective-permute-start | bytes 786440 | tf_op jit(solution)/shard_map/ppermute | solution.py:25
  200.4 1.9 reshape.30
  202.3 1.9 copy.26
  206.2 16.5 %shard_map.88 = bf16[1024,1024]{1,0:T(8,128)(2,1)} custom-call(bf16[128,4096]{1,0:T(8,128)(2,1)S(1)} %copy-done.1, bf16[128,4096]{1,0:T(8,128)(2,1)} %collective-permute-done.refs_1_, bf16[128,4096]{1,0:T(8,128)(2,1)} %collective-permute-done.1.refs_2_, bf16[64,4096]{1,0:T(8,128)(2,1)} %collective-permute-done.2.refs_3_, ...), custom_call_target="tpu_custom_call" | custom-call | flops 8589934592 | bytes 18874368 | tf_op jit(solution)/shard_map/pallas_call | solution.py:102
  (73 shorter events, 24.9 us)
Async XLA Ops:
  7.2 4.8 %copy-start = (bf16[1024,1024]{1,0:T(8,128)(2,1)S(1)}, bf16[1024,1024]{1,0:T(8,128)(2,1)}, u32[]{:S(2)}) copy-start(bf16[1024,1024]{1,0:T(8,128)(2,1)} %param.6) | copy-start | bytes 6291460
  7.2 4.8 %copy-start.5 = (bf16[1024,64]{0,1:T(8,128)(2,1)S(1)}, bf16[1024,64]{0,1:T(8,128)(2,1)}, u32[]{:S(2)}) copy-start(bf16[1024,64]{0,1:T(8,128)(2,1)} %param.10) | copy-start | bytes 393220
  7.2 198.1 %all-gather.2.cloned.1.call-start = ((), (), s32[]{:S(2)}) async-start(), calls=%async_computation.3 | async-start | bytes 8650752 | tf_op jit(solution)/shard_map/all_gather | solution.py:147
  45.8 6.1 %copy-start.1 = (bf16[128,4096]{1,0:T(8,128)(2,1)S(1)}, bf16[128,4096]{1,0:T(8,128)(2,1)}, u32[]{:S(2)}) copy-start(bf16[128,4096]{1,0:T(8,128)(2,1)} %refs_0_.1) | copy-start | bytes 3145732
  54.0 102.7 %all-to-all-start.1 = ((f32[32,80,128]{2,1,0:T(8,128)}), f32[32,80,128]{2,1,0:T(8,128)}, u32[]{:S(2)}, u32[]{:S(2)}) async-start(f32[32,80,128]{2,1,0:T(8,128)} %pad_maximum_fusion), calls=%async_computation.1 | async-start | bytes 2621440 | tf_op jit(solution)/shard_map/all_to_all | solution.py:185
  66.1 71.7 %collective-permute-start.9 = (bf16[64,4096]{1,0:T(8,128)(2,1)S(1)}, bf16[64,4096]{1,0:T(8,128)(2,1)}, u32[]{:S(2)}, u32[]{:S(2)}) collective-permute-start(bf16[64,4096]{1,0:T(8,128)(2,1)S(1)} %get-tuple-element.9), channel_id=1, source_target_pairs={{0,1},{1,0},{2,3},{3,2},{4,5},{5,4},{6,7},{7,6},{8,9},{9,8},{10,11... | collective-permute-start | bytes 1572872 | tf_op jit(solution)/shard_map/ppermute | solution.py:21
  66.1 101.0 %collective-permute-start = (bf16[128,4096]{1,0:T(8,128)(2,1)S(1)}, bf16[128,4096]{1,0:T(8,128)(2,1)}, u32[]{:S(2)}, u32[]{:S(2)}) collective-permute-start(bf16[128,4096]{1,0:T(8,128)(2,1)S(1)} %copy-done.1), channel_id=1, source_target_pairs={{0,2},{1,3},{2,4},{3,5},{4,6},{5,7},{6,0},{7,1},{8,10},{9,11},{10,... | collective-permute-start | bytes 3145736 | tf_op jit(solution)/shard_map/ppermute | solution.py:25
  66.1 103.4 %collective-permute-start.1 = (bf16[128,4096]{1,0:T(8,128)(2,1)S(1)}, bf16[128,4096]{1,0:T(8,128)(2,1)}, u32[]{:S(2)}, u32[]{:S(2)}) collective-permute-start(bf16[128,4096]{1,0:T(8,128)(2,1)S(1)} %copy-done.1), channel_id=1, source_target_pairs={{0,6},{1,7},{2,0},{3,1},{4,2},{5,3},{6,4},{7,5},{8,14},{9,15},{10,... | collective-permute-start | bytes 3145736 | tf_op jit(solution)/shard_map/ppermute | solution.py:25
  68.7 90.7 %collective-permute-start.4 = (bf16[64,4096]{1,0:T(8,128)(2,1)}, bf16[64,4096]{1,0:T(8,128)(2,1)}, u32[]{:S(2)}, u32[]{:S(2)}) collective-permute-start(bf16[64,4096]{1,0:T(8,128)(2,1)} %get-tuple-element.10), channel_id=1, source_target_pairs={{0,1},{1,0},{2,3},{3,2},{4,5},{5,4},{6,7},{7,6},{8,9},{9,8},{10,11... | collective-permute-start | bytes 1572872 | tf_op jit(solution)/shard_map/ppermute | solution.py:21
  137.8 21.8 %collective-permute-start.10 = (bf16[64,4096]{1,0:T(8,128)(2,1)}, bf16[64,4096]{1,0:T(8,128)(2,1)}, u32[]{:S(2)}, u32[]{:S(2)}) collective-permute-start(bf16[64,4096]{1,0:T(8,128)(2,1)} %collective-permute-done.9.refs_10_), channel_id=1, source_target_pairs={{0,2},{1,3},{2,4},{3,5},{4,6},{5,7},{6,0},{7,1},{8,10},{9,11},{10,... | collective-permute-start | bytes 1572872 | tf_op jit(solution)/shard_map/ppermute | solution.py:25
  139.1 34.9 %collective-permute-start.11 = (bf16[64,4096]{1,0:T(8,128)(2,1)}, bf16[64,4096]{1,0:T(8,128)(2,1)}, u32[]{:S(2)}, u32[]{:S(2)}) collective-permute-start(bf16[64,4096]{1,0:T(8,128)(2,1)} %collective-permute-done.9.refs_10_), channel_id=1, source_target_pairs={{0,6},{1,7},{2,0},{3,1},{4,2},{5,3},{6,4},{7,5},{8,14},{9,15},{10,... | collective-permute-start | bytes 1572872 | tf_op jit(solution)/shard_map/ppermute | solution.py:25
  159.5 6.8 %collective-permute-start.14 = (f32[64,128]{1,0:T(8,128)S(1)}, f32[64,128]{1,0:T(8,128)S(1)}, u32[]{:S(2)}, u32[]{:S(2)}) collective-permute-start(f32[64,128]{1,0:T(8,128)S(1)} %slice.58), channel_id=1, source_target_pairs={{0,1},{1,0},{2,3},{3,2},{4,5},{5,4},{6,7},{7,6},{8,9},{9,8},{10,11... | collective-permute-start | bytes 98312 | tf_op jit(solution)/shard_map/ppermute | solution.py:21
  159.6 26.9 %collective-permute-start.5 = (bf16[64,4096]{1,0:T(8,128)(2,1)}, bf16[64,4096]{1,0:T(8,128)(2,1)}, u32[]{:S(2)}, u32[]{:S(2)}) collective-permute-start(bf16[64,4096]{1,0:T(8,128)(2,1)} %collective-permute-done.4.refs_5_), channel_id=1, source_target_pairs={{0,2},{1,3},{2,4},{3,5},{4,6},{5,7},{6,0},{7,1},{8,10},{9,11},{10,... | collective-permute-start | bytes 1572872 | tf_op jit(solution)/shard_map/ppermute | solution.py:25
  166.2 25.8 %collective-permute-start.6 = (bf16[64,4096]{1,0:T(8,128)(2,1)}, bf16[64,4096]{1,0:T(8,128)(2,1)}, u32[]{:S(2)}, u32[]{:S(2)}) collective-permute-start(bf16[64,4096]{1,0:T(8,128)(2,1)} %collective-permute-done.4.refs_5_), channel_id=1, source_target_pairs={{0,6},{1,7},{2,0},{3,1},{4,2},{5,3},{6,4},{7,5},{8,14},{9,15},{10,... | collective-permute-start | bytes 1572872 | tf_op jit(solution)/shard_map/ppermute | solution.py:25
  167.0 11.4 %copy-start.6 = (f32[64,128]{1,0:T(8,128)}, f32[64,128]{1,0:T(8,128)S(1)}, u32[]{:S(2)}) copy-start(f32[64,128]{1,0:T(8,128)S(1)} %slice_add_fusion) | copy-start | bytes 98308
  167.0 11.4 %collective-permute-start.15 = (f32[64,128]{1,0:T(8,128)S(1)}, f32[64,128]{1,0:T(8,128)S(1)}, u32[]{:S(2)}, u32[]{:S(2)}) collective-permute-start(f32[64,128]{1,0:T(8,128)S(1)} %slice_add_fusion), channel_id=1, source_target_pairs={{0,2},{1,3},{2,0},{3,1},{4,6},{5,7},{6,4},{7,5},{8,10},{9,11},{10,... | collective-permute-start | bytes 98312 | tf_op jit(solution)/shard_map/ppermute | solution.py:126
  169.5 25.3 %collective-permute-start.12 = (bf16[32,4096]{1,0:T(8,128)(2,1)}, bf16[32,4096]{1,0:T(8,128)(2,1)}, u32[]{:S(2)}, u32[]{:S(2)}) collective-permute-start(bf16[32,4096]{1,0:T(8,128)(2,1)} %slice.53), channel_id=1, source_target_pairs={{0,2},{1,3},{2,4},{3,5},{4,6},{5,7},{6,0},{7,1},{8,10},{9,11},{10,... | collective-permute-start | bytes 786440 | tf_op jit(solution)/shard_map/ppermute | solution.py:25
  174.0 31.2 %collective-permute-start.2 = (bf16[64,4096]{1,0:T(8,128)(2,1)}, bf16[64,4096]{1,0:T(8,128)(2,1)}, u32[]{:S(2)}, u32[]{:S(2)}) collective-permute-start(bf16[64,4096]{1,0:T(8,128)(2,1)} %slice.49), channel_id=1, source_target_pairs={{0,2},{1,3},{2,4},{3,5},{4,6},{5,7},{6,0},{7,1},{8,10},{9,11},{10,... | collective-permute-start | bytes 1572872 | tf_op jit(solution)/shard_map/ppermute | solution.py:25
  178.5 26.8 %collective-permute-start.3 = (bf16[64,4096]{1,0:T(8,128)(2,1)}, bf16[64,4096]{1,0:T(8,128)(2,1)}, u32[]{:S(2)}, u32[]{:S(2)}) collective-permute-start(bf16[64,4096]{1,0:T(8,128)(2,1)} %slice.50), channel_id=1, source_target_pairs={{0,6},{1,7},{2,0},{3,1},{4,2},{5,3},{6,4},{7,5},{8,14},{9,15},{10,... | collective-permute-start | bytes 1572872 | tf_op jit(solution)/shard_map/ppermute | solution.py:25
  179.8 20.6 %all-to-all-start.2 = ((f32[32,16,128]{2,1,0:T(8,128)}), f32[32,16,128]{2,1,0:T(8,128)}, u32[]{:S(2)}, u32[]{:S(2)}) async-start(f32[32,16,128]{2,1,0:T(8,128)} %broadcast_in_dim.20), calls=%async_computation.2 | async-start | bytes 524288 | tf_op jit(solution)/shard_map/all_to_all | solution.py:191
  187.1 8.1 %collective-permute-start.16 = (f32[64,128]{1,0:T(8,128)S(1)}, f32[64,128]{1,0:T(8,128)S(1)}, u32[]{:S(2)}, u32[]{:S(2)}) collective-permute-start(f32[64,128]{1,0:T(8,128)S(1)} %add.10), channel_id=1, source_target_pairs={{0,6},{1,7},{2,4},{3,5},{4,2},{5,3},{6,0},{7,1},{8,14},{9,15},{10,... | collective-permute-start | bytes 98312 | tf_op jit(solution)/shard_map/ppermute | solution.py:126
  192.0 12.2 %collective-permute-start.13 = (bf16[32,4096]{1,0:T(8,128)(2,1)}, bf16[32,4096]{1,0:T(8,128)(2,1)}, u32[]{:S(2)}, u32[]{:S(2)}) collective-permute-start(bf16[32,4096]{1,0:T(8,128)(2,1)} %slice.54), channel_id=1, source_target_pairs={{0,6},{1,7},{2,0},{3,1},{4,2},{5,3},{6,4},{7,5},{8,14},{9,15},{10,... | collective-permute-start | bytes 786440 | tf_op jit(solution)/shard_map/ppermute | solution.py:25
  194.8 9.4 %collective-permute-start.7 = (bf16[32,4096]{1,0:T(8,128)(2,1)}, bf16[32,4096]{1,0:T(8,128)(2,1)}, u32[]{:S(2)}, u32[]{:S(2)}) collective-permute-start(bf16[32,4096]{1,0:T(8,128)(2,1)} %slice.51), channel_id=1, source_target_pairs={{0,2},{1,3},{2,4},{3,5},{4,6},{5,7},{6,0},{7,1},{8,10},{9,11},{10,... | collective-permute-start | bytes 786440 | tf_op jit(solution)/shard_map/ppermute | solution.py:25
  195.8 9.4 %collective-permute-start.8 = (bf16[32,4096]{1,0:T(8,128)(2,1)}, bf16[32,4096]{1,0:T(8,128)(2,1)}, u32[]{:S(2)}, u32[]{:S(2)}) collective-permute-start(bf16[32,4096]{1,0:T(8,128)(2,1)} %slice.52), channel_id=1, source_target_pairs={{0,6},{1,7},{2,0},{3,1},{4,2},{5,3},{6,4},{7,5},{8,14},{9,15},{10,... | collective-permute-start | bytes 786440 | tf_op jit(solution)/shard_map/ppermute | solution.py:25
  (6 other events, 4.6 us)
Sparse Core Ops, SparseCore 0:
  10.1 150.2 all-gather.1

commit v2 on v0

v2 whole, which is shorter than its diff:
```python
import functools

import jax
import jax.numpy as jnp
from jax import lax
from jax.experimental import pallas as pl
from jax.experimental.pallas import tpu as pltpu
from jax.sharding import PartitionSpec as P

BLOCK = 128
NX, NY, NZ = 4, 4, 4
STEPS = (0, 1, -1, 2)
ROWS = 128
M_TILE = 256
COST = 40 * 10**9

adapter_scale = 2.0
loss_scale_factor = 64.0


def hi_swap(value):
    return lax.ppermute(value, "tensor", [(t, t ^ 1) for t in range(2 * NX)])


def x_shift(value, step):
    return lax.ppermute(
        value,
        "tensor",
        [(t, ((t // 2 + step) % NX) * 2 + t % 2) for t in range(2 * NX)],
    )


def core_swap(value):
    return lax.ppermute(value, "dp", [(d, d ^ 1) for d in range(2 * NY * NZ)])


def z_shift(value, step):
    pairs = []
    for d in range(2 * NY * NZ):
        y, z, c = d // (2 * NZ), d // 2 % NZ, d % 2
        pairs.append((d, (y * NZ + (z + step) % NZ) * 2 + c))
    return lax.ppermute(value, "dp", pairs)


def y_shift(value, step):
    n = 2 * NY * NZ
    return lax.ppermute(value, "dp", [(d, (d + step * 2 * NZ) % n) for d in range(n)])


def ring_places(flip, base):
    return [(flip, dx, base) for dx in (0, -1, 1, 2)]


def product_kernel(places, sizes, fresh, *refs):
    count = len(places)
    pieces, projected, down = refs[:count], refs[count], refs[count + 1]
    if fresh:
        blocks = refs[count + 2 : count + 2 + 2 * NY]
        out, ordered, *scratch = refs[count + 2 + 2 * NY :]
    else:
        ordered, _, out, *scratch = refs[count + 2 :]
    w_all, g_all, p_all, o_all, w_sem, g_sem, o_sem, h_sem = scratch
    tensor, group = lax.axis_index("tensor"), lax.axis_index("dp")
    x, hi = tensor // 2, lax.rem(tensor, 2)
    y, z, core = group // (2 * NZ), lax.rem(group // 2, NZ), lax.rem(group, 2)
    tokens, depth = g_all.shape
    k_chunk = depth // NY
    starts = [sum(sizes[:p]) for p in range(count)]

    def token(p):
        flip, dx, start = places[p]
        other = lax.rem(x + dx + NX, NX) * 2 + (1 - hi if flip else hi)
        return pl.multiple_of(other * ROWS + start, sizes[p])

    def piece_copy(p):
        return pltpu.make_async_copy(
            pieces[p], g_all.at[pl.ds(starts[p], sizes[p])], g_sem.at[p]
        )

    def weight_rows(k):
        if not fresh:
            return k * k_chunk
        return pl.multiple_of(lax.rem(y + STEPS[k] + NY, NY) * k_chunk, k_chunk)

    def weight_copies(k):
        if not fresh:
            rows = pl.ds(k * k_chunk, k_chunk)
            yield pltpu.make_async_copy(ordered.at[rows], w_all.at[rows], h_sem.at[k])
            return
        for c in range(2):
            for q in range(NZ):
                zz = lax.rem(z + STEPS[q] + NZ, NZ)
                at = weight_rows(k) + (zz * 2 + (1 - core if c else core)) * BLOCK
                yield pltpu.make_async_copy(
                    blocks[2 * k + c].at[pl.ds(q * BLOCK, BLOCK)],
                    w_all.at[pl.ds(pl.multiple_of(at, BLOCK), BLOCK)],
                    w_sem.at[k, c * NZ + q],
                )

    def out_copy(p):
        return pltpu.make_async_copy(
            o_all.at[pl.ds(starts[p], sizes[p])], out.at[pl.ds(token(p), sizes[p])], o_sem.at[p]
        )

    first = [p for p in range(count) if starts[p] < M_TILE]
    for p in first:
        piece_copy(p).start()
    for k in range(NY):
        for copy in weight_copies(k):
            copy.start()
    for p in range(count):
        if p not in first:
            piece_copy(p).start()
        p_all[starts[p] : starts[p] + sizes[p], :] = projected[pl.ds(token(p), sizes[p]), :]

    for tile in range(tokens // M_TILE):
        low, high = tile * M_TILE, (tile + 1) * M_TILE
        rows = slice(low, high)
        inside = [p for p in range(count) if low <= starts[p] < high]
        for p in inside:
            piece_copy(p).wait()
        total = adapter_scale * jnp.dot(
            p_all[rows, :], down[...], preferred_element_type=jnp.float32
        )
        if tile == 0:
            for k in range(NY):
                for copy in weight_copies(k):
                    copy.wait()
                columns = pl.ds(weight_rows(k), k_chunk)
                total += jnp.dot(
                    g_all[rows, columns], w_all[columns, :], preferred_element_type=jnp.float32
                )
            if fresh:
                pltpu.make_async_copy(w_all, ordered, h_sem.at[0]).start()
        else:
            total += jnp.dot(g_all[rows, :], w_all[...], preferred_element_type=jnp.float32)
        o_all[rows, :] = total.astype(o_all.dtype)
        for p in inside:
            out_copy(p).start()
    for p in range(count):
        out_copy(p).wait()
    if fresh:
        pltpu.make_async_copy(w_all, ordered, h_sem.at[0]).wait()


def product(gathered, projected, down, blocks=None, weights=None, held=None):
    pieces = [piece for values, _ in gathered for piece in values]
    places = [place for _, values in gathered for place in values]
    sizes = [piece.shape[0] for piece in pieces]
    tokens, width = sum(sizes), down.shape[1]
    depth, rank = pieces[0].shape[1], projected.shape[1]
    fresh = blocks is not None
    whole = pl.BlockSpec(memory_space=pltpu.VMEM)
    outside = pl.BlockSpec(memory_space=pl.ANY)
    operands = [*pieces, projected, down]
    specs = [outside] * len(pieces) + [whole, whole]
    result = jax.ShapeDtypeStruct((projected.shape[0], width), jnp.bfloat16)
    scratch = [
        pltpu.VMEM((depth, width), jnp.bfloat16),
        pltpu.VMEM((tokens, depth), jnp.bfloat16),
        pltpu.VMEM((tokens, rank), jnp.bfloat16),
        pltpu.VMEM((tokens, width), jnp.bfloat16),
        pltpu.SemaphoreType.DMA((NY, 2 * NZ)),
        pltpu.SemaphoreType.DMA((len(pieces),)),
        pltpu.SemaphoreType.DMA((len(pieces),)),
        pltpu.SemaphoreType.DMA((NY,)),
    ]
    if fresh:
        operands += blocks
        specs += [outside] * len(blocks)
        outs, out_specs = (result, jax.ShapeDtypeStruct((depth, width), jnp.bfloat16)), (outside, outside)
        aliases = {}
    else:
        aliases = {len(operands) + 1: 0}
        operands += [weights, held]
        specs += [outside, outside]
        outs, out_specs = result, outside
    return pl.pallas_call(
        functools.partial(product_kernel, places, sizes, fresh),
        out_shape=outs,
        in_specs=specs,
        out_specs=out_specs,
        input_output_aliases=aliases,
        scratch_shapes=scratch,
        compiler_params=pltpu.CompilerParams(vmem_limit_bytes=56 * 1024 * 1024),
        cost_estimate=pl.CostEstimate(
            flops=4 * tokens * width * depth,
            bytes_accessed=2 * (tokens + width) * depth + 2 * tokens * width,
            transcendentals=0,
        ),
    )(*operands)


def local(kernel, outs, flops, *operands):
    return pl.pallas_call(
        kernel,
        out_shape=outs,
        in_specs=[pl.BlockSpec(memory_space=pltpu.VMEM)] * len(operands),
        out_specs=jax.tree.map(lambda _: pl.BlockSpec(memory_space=pltpu.VMEM), outs),
        compiler_params=pltpu.CompilerParams(vmem_limit_bytes=24 * 1024 * 1024),
        cost_estimate=pl.CostEstimate(flops=flops, bytes_accessed=8 * 2**20, transcendentals=0),
    )(*operands)


def dot(left, right, left_dim, right_dim):
    return lax.dot_general(
        left, right, (((left_dim,), (right_dim,)), ((), ())), preferred_element_type=jnp.float32
    )


def first_kernel(attention, down_t, gradient, up, parcel):
    rank = down_t.shape[0]
    projected = dot(gradient[...], up[...], 1, 1).astype(parcel.dtype)
    partial = dot(attention[...], down_t[...], 1, 1).astype(parcel.dtype)
    for t in range(parcel.shape[0]):
        parcel[t, :, :rank] = partial[t * ROWS : (t + 1) * ROWS]
        parcel[t, :, rank:] = projected


def second_kernel(arrived, attention, gradient, parcel, projected):
    rank = projected.shape[1]
    sources = arrived.shape[0]
    adapted = arrived[0, :, :rank].astype(jnp.float32)
    for t in range(1, sources):
        adapted += arrived[t, :, :rank].astype(jnp.float32)
    for t in range(sources):
        projected[t * ROWS : (t + 1) * ROWS, :] = arrived[t, :, rank:]
    up_term = dot(adapted.astype(gradient.dtype), gradient[...], 0, 0).astype(parcel.dtype)
    down_term = dot(projected[...], attention[...], 0, 0).astype(parcel.dtype)
    across = down_term.shape[1] // 128
    for d in range(parcel.shape[0]):
        parcel[d, :rank, :] = up_term[:, d * 128 : (d + 1) * 128]
        a, b = d // across, d % across
        parcel[d, rank:, :] = down_term[a * 16 : (a + 1) * 16, b * 128 : (b + 1) * 128]


def third_kernel(factor, arrived, up_parcel, down_parcel):
    rank = up_parcel.shape[0]
    total = arrived[0].astype(jnp.float32)
    for d in range(1, arrived.shape[0]):
        total += arrived[d].astype(jnp.float32)
    total *= factor
    up_parcel[...] = total[:rank]
    for d in range(down_parcel.shape[0]):
        down_parcel[d] = total[rank:]


def body(
    attention_output,
    output_gradient,
    codes,
    block_scale_values,
    adapter_down_factor,
    adapter_up_factor,
):
    f32, bf16 = jnp.float32, jnp.bfloat16
    n_dp, n_tensor = lax.axis_size("dp"), lax.axis_size("tensor")
    rank = adapter_down_factor.shape[1]
    down_t = adapter_down_factor.T
    half = ROWS // 2
    stage = lax.optimization_barrier

    scaled = (codes.astype(f32) * jnp.repeat(block_scale_values, BLOCK, axis=0)).astype(bf16).T
    own_before, own_behind = x_shift(output_gradient, 1), x_shift(output_gradient, -1)
    z_blocks = [scaled] + [z_shift(scaled, -step) for step in STEPS[1:]]
    parcel = local(
        first_kernel,
        jax.ShapeDtypeStruct((n_tensor, ROWS, 2 * rank), bf16),
        COST,
        attention_output, down_t, output_gradient, adapter_up_factor,
    )
    parcel = lax.all_to_all(parcel, "tensor", 0, 0, tiled=True)
    mine = jnp.concatenate(z_blocks, axis=0)
    top, bottom, whole = output_gradient[:half], output_gradient[half:], output_gradient

    mine, top, bottom, whole, own_before, own_behind = stage(
        (mine, top, bottom, whole, own_before, own_behind)
    )
    first = hi_swap(top)
    own_far = x_shift(whole, 2)
    y_blocks = [mine] + [y_shift(mine, -step) for step in STEPS[1:3]]
    mine_swapped = core_swap(mine)
    parcel, projected = local(
        second_kernel,
        (
            jax.ShapeDtypeStruct((n_dp, rank + 16, 128), bf16),
            jax.ShapeDtypeStruct((n_tensor * ROWS, rank), bf16),
        ),
        COST,
        parcel, attention_output, output_gradient,
    )
    parcel = lax.all_to_all(parcel, "dp", 0, 0, tiled=True)

    first, own_far, mine, mine_swapped, bottom, projected, *y_blocks = stage(
        (first, own_far, mine, mine_swapped, bottom, projected, *y_blocks)
    )
    second = hi_swap(bottom)
    first_ring = [first, x_shift(first, 1), x_shift(first, -1), x_shift(first, 2)]
    y_blocks.append(y_shift(mine, -STEPS[3]))

    second, *rest = stage((second, *first_ring, *y_blocks))
    first_ring, y_blocks = rest[:4], rest[4:]
    blocks = [y_blocks[0], mine_swapped]
    for block in y_blocks[1:]:
        blocks += [block, core_swap(block)]
    second_ring = [second, x_shift(second, 1), x_shift(second, -1), x_shift(second, 2)]
    own_ring = [output_gradient, own_before, own_behind, own_far]
    input_gradient, weights = product(
        [(own_ring, ring_places(0, 0)), (first_ring, ring_places(1, 0))],
        projected, down_t, blocks=blocks,
    )
    parcel, input_gradient = stage((parcel, input_gradient))
    up_parcel, down_parcel = local(
        functools.partial(third_kernel, adapter_scale / loss_scale_factor),
        (
            jax.ShapeDtypeStruct((rank, 128), f32),
            jax.ShapeDtypeStruct((n_dp, 16, 128), f32),
        ),
        10**8,
        parcel,
    )
    down_parcel = lax.all_to_all(down_parcel, "dp", 0, 0, tiled=True)
    up_part = (up_parcel + x_shift(up_parcel, 2)) + (
        x_shift(up_parcel, 1) + x_shift(up_parcel, -1)
    )

    up_part, input_gradient, *second_ring = stage((up_part, input_gradient, *second_ring))
    up_factor_gradient = up_part + hi_swap(up_part)
    down_factor_gradient = (
        down_parcel.reshape(rank // 16, -1, 16, 128).transpose(0, 2, 1, 3).reshape(rank, -1).T
    )
    input_gradient = product(
        [(second_ring, ring_places(1, half))],
        projected, down_t, weights=weights, held=input_gradient,
    )
    return (input_gradient, down_factor_gradient, up_factor_gradient)


def solution(mesh):
    placed = (
        P("dp", "tensor"),
        P(("dp", "tensor"), None),
        P("tensor", "dp"),
        P("tensor", "dp"),
        P("tensor", None),
        P(),
    )
    return jax.shard_map(
        body,
        mesh=mesh,
        in_specs=placed,
        out_specs=(P("dp", "tensor"), P("tensor", None), P(None, "dp")),
        check_vma=False,
    )
```

time: 734 us -> 160 us (0.22)
  waiting for transfers between devices: 490 us -> 54 us
  blocking collectives: 180 us -> 0 us
  starting transfers between devices: 0.16 us -> 66.1 us
  matrix products: 29.8 us -> 0 us
  Pallas kernels: 0 us -> 25.7 us
  between operations: 13.8 us -> 0.84 us
  other arithmetic: 9.31 us -> 1.85 us
    psum x1 -> x0, waiting for transfers between devices: 248 us -> none  [body(): down_factor_gradient = lax.psum(down_factor_term, 'dp')]
    reduce_scatter x1 -> x0, waiting for transfers between devices: 142 us -> none  [body(): lax.psum_scatter(adapter_term, 'dp', scatter_dimension=1, tiled=True)]
    psum x1 -> x0, blocking collectives: 127 us -> none  [body(): adapter_output = lax.psum(partial_result, 'tensor').astype(jnp.bfloat16)]
    all_gather x2 -> x0, waiting for transfers between devices: 99.1 us -> none  [the longest x1 71.3 us: body(): lax.all_gather(codes.astype(jnp.float32), 'dp', axis=1, tiled=True)]
    all_gather x1 -> x0, blocking collectives: 53.1 us -> none  [body(): lax.all_gather(column_scales, 'dp', axis=1, tiled=True)]
    ppermute x0 -> x25, waiting for transfers between devices: none -> 49.9 us  [the longest x12 27.9 us: x_shift(): lax.ppermute(value, 'tensor', [(t, (t // 2 + step) % NX * 2 + t % 2) for...]
    ppermute x0 -> x25, starting transfers between devices: none -> 43.6 us  [the longest x12 15.9 us: x_shift(): lax.ppermute(value, 'tensor', [(t, (t // 2 + step) % NX * 2 + t % 2) for...]
    dot_general x6 -> x0, matrix products: 29.8 us -> none  [the longest x1 12.7 us: body(): lax.dot_general(gradient_complete, scaled.astype(jnp.bfloat16), (((1,), (...]
  transfers between devices with their start and end apart: 4 -> 28, of which waited for: 4 -> 8; matrix products, arithmetic and copies ran while one was open for 6% -> 2% of each run, Pallas kernels for 0% -> 16%
where the time goes in v2:
time: 160 us; the launch traced here: 159 us
  starting transfers between devices  66.1 us (41%)
  waiting for transfers between devices  54 us (34%)
  Pallas kernels  25.7 us (16%)
  local copies, waits for them, and re-layouts  10.7 us (7%)
  other arithmetic  1.85 us (1%)
    ppermute x12, waiting for transfers between devices, x_shift(): lax.ppermute(value, 'tensor', [(t, (t // 2 + step) % NX * 2 + t % 2) for...  27.9 us
    ppermute x3, waiting for transfers between devices, hi_swap(): return lax.ppermute(value, 'tensor', [(t, t ^ 1) for t in range(2 * NX)])  22 us
    pallas_call x2, Pallas kernels, product(): pl.pallas_call(functools.partial(product_kernel, places, sizes, fresh), o...  21.6 us
    ppermute x12, starting transfers between devices, x_shift(): lax.ppermute(value, 'tensor', [(t, (t // 2 + step) % NX * 2 + t % 2) for...  15.9 us
    unnamed x34, local copies, waits for them, and re-layouts  9.67 us
    ppermute x4, starting transfers between devices, core_swap(): return lax.ppermute(value, 'dp', [(d, d ^ 1) for d in range(2 * NY * NZ)])  8.54 us
    all_to_all x1, starting transfers between devices, body(): down_parcel = lax.all_to_all(down_parcel, 'dp', 0, 0, tiled=True)  8.06 us
    ppermute x3, starting transfers between devices, hi_swap(): return lax.ppermute(value, 'tensor', [(t, t ^ 1) for t in range(2 * NX)])  7.89 us
  transfers between devices with their start and end apart: 28, of which 8 were waited for; matrix products, arithmetic and copies ran while one was open for 2% of the time, Pallas kernels for 16%

profile of v2, /device:TPU:1, one launch (start us, length us, event | category | flops | bytes accessed | tf_op | source)
XLA Modules:
  0.0 159.2 jit_solution(17278133614914856503)
XLA Ops:
  1.9 3.9 %collective-permute-start.2 = (bf16[128,1024]{1,0:T(8,128)(2,1)S(1)}, bf16[128,1024]{1,0:T(8,128)(2,1)S(1)}, u32[]{:S(2)}, u32[]{:S(2)}) collective-permute-start(bf16[128,1024]{1,0:T(8,128)(2,1)S(1)} %fusion), channel_id=1, source_target_pairs={{0,32},{8,40},{16,48},{24,56},{32,0},{40,8},{48,16},{56,24},{64,96... | collective-permute-start | bytes 786440 | tf_op jit(solution)/shard_map/ppermute | solution.py:42
  5.8 1.6 %collective-permute-start.1 = (bf16[128,1024]{1,0:T(8,128)(2,1)S(1)}, bf16[128,1024]{1,0:T(8,128)(2,1)S(1)}, u32[]{:S(2)}, u32[]{:S(2)}) collective-permute-start(bf16[128,1024]{1,0:T(8,128)(2,1)S(1)} %fusion), channel_id=1, source_target_pairs={{0,16},{8,24},{16,32},{24,40},{32,48},{40,56},{48,0},{56,8},{64,80... | collective-permute-start | bytes 786440 | tf_op jit(solution)/shard_map/ppermute | solution.py:42
  16.5 1.7 %shard_map.88 = bf16[8,128,128]{2,1,0:T(8,128)(2,1)} custom-call(bf16[1024,1024]{1,0:T(8,128)(2,1)S(1)} %copy-done.3, bf16[64,1024]{1,0:T(8,128)(2,1)S(1)} %bitcast.20, bf16[128,4096]{1,0:T(8,128)(2,1)S(1)} %copy-done.1, bf16[64,4096]{1,0:T(8,128)(2,1)S(1)} %copy-done.5), custom_call_target="tpu_custom_call" | custom-call | flops 40000000000 | bytes 8388608 | tf_op jit(solution)/shard_map/pallas_call | solution.py:195
  18.2 7.6 %all-to-all-start = ((bf16[8,128,128]{2,1,0:T(8,128)(2,1)}), bf16[8,128,128]{2,1,0:T(8,128)(2,1)S(1)}, u32[]{:S(2)}, u32[]{:S(2)}) async-start(bf16[8,128,128]{2,1,0:T(8,128)(2,1)} %shard_map.88), calls=%async_computation | async-start | bytes 524288 | tf_op jit(solution)/shard_map/all_to_all | solution.py:272
  28.6 5.1 %collective-permute-done.3.refs_1_ = bf16[128,4096]{1,0:T(8,128)(2,1)} collective-permute-done((bf16[128,4096]{1,0:T(8,128)(2,1)}, bf16[128,4096]{1,0:T(8,128)(2,1)}, u32[]{:S(2)}, u32[]{:S(2)}) %collective-permute-start.3) | collective-permute-done | bytes 1048608 | tf_op jit(solution)/shard_map/ppermute | solution.py:26
  33.7 4.5 %collective-permute-start.7 = (bf16[512,1024]{1,0:T(8,128)(2,1)S(1)}, bf16[512,1024]{1,0:T(8,128)(2,1)}, u32[]{:S(2)}, u32[]{:S(2)}) collective-permute-start(bf16[512,1024]{1,0:T(8,128)(2,1)S(1)} %pad_maximum_fusion.refs_10_), channel_id=1, source_target_pairs={{0,8},{8,0},{16,24},{24,16},{32,40},{40,32},{48,56},{56,48},{64,72... | collective-permute-start | bytes 3145736 | tf_op jit(solution)/shard_map/ppermute | solution.py:34
  38.3 2.7 %collective-permute-start.8 = (bf16[512,1024]{1,0:T(8,128)(2,1)S(1)}, bf16[512,1024]{1,0:T(8,128)(2,1)}, u32[]{:S(2)}, u32[]{:S(2)}) collective-permute-start(bf16[512,1024]{1,0:T(8,128)(2,1)S(1)} %pad_maximum_fusion.refs_10_), channel_id=1, source_target_pairs={{0,192},{8,200},{16,208},{24,216},{32,224},{40,232},{48,240},{56,2... | collective-permute-start | bytes 3145736 | tf_op jit(solution)/shard_map/ppermute | solution.py:47
  41.0 5.1 %collective-permute-start.5 = (bf16[64,4096]{1,0:T(8,128)(2,1)}, bf16[64,4096]{1,0:T(8,128)(2,1)}, u32[]{:S(2)}, u32[]{:S(2)}) collective-permute-start(bf16[64,4096]{1,0:T(8,128)(2,1)} %get-tuple-element.44), channel_id=1, source_target_pairs={{0,1},{1,0},{2,3},{3,2},{4,5},{5,4},{6,7},{7,6},{8,9},{9,8},{10,11... | collective-permute-start | bytes 1572872 | tf_op jit(solution)/shard_map/ppermute | solution.py:22
  46.1 2.4 %collective-permute-start.6 = (bf16[128,4096]{1,0:T(8,128)(2,1)S(1)}, bf16[128,4096]{1,0:T(8,128)(2,1)}, u32[]{:S(2)}, u32[]{:S(2)}) collective-permute-start(bf16[128,4096]{1,0:T(8,128)(2,1)S(1)} %copy-done.2), channel_id=1, source_target_pairs={{0,4},{1,5},{2,6},{3,7},{4,0},{5,1},{6,2},{7,3},{8,12},{9,13},{10,... | collective-permute-start | bytes 3145736 | tf_op jit(solution)/shard_map/ppermute | solution.py:26
  50.2 1.7 %shard_map.89 = (bf16[32,80,128]{2,1,0:T(8,128)(2,1)}, bf16[1024,64]{1,0:T(8,128)(2,1)S(1)}) custom-call(bf16[8,128,128]{2,1,0:T(8,128)(2,1)S(1)} %all-to-all-done.arrived, bf16[1024,1024]{1,0:T(8,128)(2,1)S(1)} %copy-done.4, bf16[128,4096]{1,0:T(8,128)(2,1)S(1)} %copy-done.2), custom_call_target="tpu_custom_call" | custom-call | flops 40000000000 | bytes 8388608 | tf_op jit(solution)/shard_map/pallas_call | solution.py:195
  52.5 8.3 %collective-permute-done.5.refs_4_ = bf16[64,4096]{1,0:T(8,128)(2,1)} collective-permute-done((bf16[64,4096]{1,0:T(8,128)(2,1)}, bf16[64,4096]{1,0:T(8,128)(2,1)}, u32[]{:S(2)}, u32[]{:S(2)}) %collective-permute-start.5) | collective-permute-done | bytes 524320 | tf_op jit(solution)/shard_map/ppermute | solution.py:22
  60.8 11.1 %collective-permute-done.6.refs_3_ = bf16[128,4096]{1,0:T(8,128)(2,1)} collective-permute-done((bf16[128,4096]{1,0:T(8,128)(2,1)S(1)}, bf16[128,4096]{1,0:T(8,128)(2,1)}, u32[]{:S(2)}, u32[]{:S(2)}) %collective-permute-start.6) | collective-permute-done | bytes 1048608 | tf_op jit(solution)/shard_map/ppermute | solution.py:26
  77.5 13.7 %collective-permute-done.10.refs_0_ = bf16[64,4096]{1,0:T(8,128)(2,1)S(1)} collective-permute-done((bf16[64,4096]{1,0:T(8,128)(2,1)S(1)}, bf16[64,4096]{1,0:T(8,128)(2,1)S(1)}, u32[]{:S(2)}, u32[]{:S(2)}) %collective-permute-start.10) | collective-permute-done | bytes 524320 | tf_op jit(solution)/shard_map/ppermute | solution.py:22
  91.2 7.3 %collective-permute-done.13.refs_7_ = bf16[64,4096]{1,0:T(8,128)(2,1)S(1)} collective-permute-done((bf16[64,4096]{1,0:T(8,128)(2,1)}, bf16[64,4096]{1,0:T(8,128)(2,1)S(1)}, u32[]{:S(2)}, u32[]{:S(2)}) %collective-permute-start.13) | collective-permute-done | bytes 524320 | tf_op jit(solution)/shard_map/ppermute | solution.py:26
  98.5 3.5 %collective-permute-start.15 = (bf16[512,1024]{1,0:T(8,128)(2,1)}, bf16[512,1024]{1,0:T(8,128)(2,1)}, u32[]{:S(2)}, u32[]{:S(2)}) collective-permute-start(bf16[512,1024]{1,0:T(8,128)(2,1)} %collective-permute-done.8.refs_12_), channel_id=1, source_target_pairs={{0,8},{8,0},{16,24},{24,16},{32,40},{40,32},{48,56},{56,48},{64,72... | collective-permute-start | bytes 3145736 | tf_op jit(solution)/shard_map/ppermute | solution.py:34
  102.5 6.8 %all-to-all-start.1 = ((bf16[32,80,128]{2,1,0:T(8,128)(2,1)}), bf16[32,80,128]{2,1,0:T(8,128)(2,1)S(1)}, u32[]{:S(2)}, u32[]{:S(2)}) async-start(bf16[32,80,128]{2,1,0:T(8,128)(2,1)} %get-tuple-element.41), calls=%async_computation.1 | async-start | bytes 1310720 | tf_op jit(solution)/shard_map/all_to_all | solution.py:292
  110.3 1.8 %collective-permute-start.22 = (bf16[64,4096]{1,0:T(8,128)(2,1)S(1)}, bf16[64,4096]{1,0:T(8,128)(2,1)}, u32[]{:S(2)}, u32[]{:S(2)}) collective-permute-start(bf16[64,4096]{1,0:T(8,128)(2,1)S(1)} %collective-permute-done.10.refs_0_), channel_id=1, source_target_pairs={{0,6},{1,7},{2,0},{3,1},{4,2},{5,3},{6,4},{7,5},{8,14},{9,15},{10,... | collective-permute-start | bytes 1572872 | tf_op jit(solution)/shard_map/ppermute | solution.py:26
  112.6 13.4 %shard_map.90 = (bf16[1024,1024]{1,0:T(8,128)(2,1)}, bf16[4096,1024]{1,0:T(8,128)(2,1)}) custom-call(bf16[128,4096]{1,0:T(8,128)(2,1)} %refs_0_.1, bf16[128,4096]{1,0:T(8,128)(2,1)} %collective-permute-done.3.refs_1_, bf16[128,4096]{1,0:T(8,128)(2,1)} %collective-permute-done.4.refs_2_, bf16[128,4096]{1,0:T(8,128)(2,1)} %collective-permute-done.6.refs_3_, ...), custom_call_target="tpu_custom_call" | custom-call | flops 12884901888 | bytes 16252928 | tf_op jit(solution)/shard_map/pallas_call | solution.py:178
  126.0 2.9 %all-to-all-done.1.arrived = bf16[32,80,128]{2,1,0:T(8,128)(2,1)S(1)} async-done(((bf16[32,80,128]{2,1,0:T(8,128)(2,1)}), bf16[32,80,128]{2,1,0:T(8,128)(2,1)S(1)}, u32[]{:S(2)}, u32[]{:S(2)}) %all-to-all-start.1) | async-done | bytes 655392 | tf_op jit(solution)/shard_map/all_to_all | solution.py:292
  130.5 1.8 %collective-permute-start.20 = (f32[64,128]{1,0:T(8,128)S(1)}, f32[64,128]{1,0:T(8,128)S(1)}, u32[]{:S(2)}, u32[]{:S(2)}) collective-permute-start(f32[64,128]{1,0:T(8,128)S(1)} %get-tuple-element.68), channel_id=1, source_target_pairs={{0,6},{1,7},{2,0},{3,1},{4,2},{5,3},{6,4},{7,5},{8,14},{9,15},{10,... | collective-permute-start | bytes 98312 | tf_op jit(solution)/shard_map/ppermute | solution.py:26
  132.3 4.4 %collective-permute-done.19 = f32[64,128]{1,0:T(8,128)S(1)} collective-permute-done((f32[64,128]{1,0:T(8,128)S(1)}, f32[64,128]{1,0:T(8,128)S(1)}, u32[]{:S(2)}, u32[]{:S(2)}) %collective-permute-start.19) | collective-permute-done | bytes 32800 | tf_op jit(solution)/shard_map/ppermute | solution.py:26
  137.6 8.1 %all-to-all-start.2 = ((f32[32,16,128]{2,1,0:T(8,128)}), f32[32,16,128]{2,1,0:T(8,128)S(1)}, u32[]{:S(2)}, u32[]{:S(2)}) async-start(f32[32,16,128]{2,1,0:T(8,128)} %get-tuple-element.77), calls=%async_computation.2 | async-start | bytes 524288 | tf_op jit(solution)/shard_map/all_to_all | solution.py:322
  145.8 2.5 %collective-permute-start.24 = (f32[64,128]{1,0:T(8,128)S(1)}, f32[64,128]{1,0:T(8,128)S(1)}, u32[]{:S(2)}, u32[]{:S(2)}) collective-permute-start(f32[64,128]{1,0:T(8,128)S(1)} %add_add_fusion), channel_id=1, source_target_pairs={{0,1},{1,0},{2,3},{3,2},{4,5},{5,4},{6,7},{7,6},{8,9},{9,8},{10,11... | collective-permute-start | bytes 98312 | tf_op jit(solution)/shard_map/ppermute | solution.py:22
  148.3 8.3 %shard_map.92 = bf16[1024,1024]{1,0:T(8,128)(2,1)} custom-call(bf16[64,4096]{1,0:T(8,128)(2,1)} %copy-done.11, bf16[64,4096]{1,0:T(8,128)(2,1)} %copy-done.12, bf16[64,4096]{1,0:T(8,128)(2,1)} %collective-permute-done.22.refs_2_, bf16[64,4096]{1,0:T(8,128)(2,1)} %collective-permute-done.23.refs_3_, ...), custom_call_target="tpu_custom_call", output_to_operand_aliasing={{}: (7, {})} | custom-call | flops 4294967296 | bytes 11010048 | tf_op jit(solution)/shard_map/pallas_call | solution.py:178
  (78 shorter events, 28.1 us)
Async XLA Ops:
  1.9 24.8 %collective-permute-start.2 = (bf16[128,1024]{1,0:T(8,128)(2,1)S(1)}, bf16[128,1024]{1,0:T(8,128)(2,1)S(1)}, u32[]{:S(2)}, u32[]{:S(2)}) collective-permute-start(bf16[128,1024]{1,0:T(8,128)(2,1)S(1)} %fusion), channel_id=1, source_target_pairs={{0,32},{8,40},{16,48},{24,56},{32,0},{40,8},{48,16},{56,24},{64,96... | collective-permute-start | bytes 786440 | tf_op jit(solution)/shard_map/ppermute | solution.py:42
  5.8 20.9 %collective-permute-start.1 = (bf16[128,1024]{1,0:T(8,128)(2,1)S(1)}, bf16[128,1024]{1,0:T(8,128)(2,1)S(1)}, u32[]{:S(2)}, u32[]{:S(2)}) collective-permute-start(bf16[128,1024]{1,0:T(8,128)(2,1)S(1)} %fusion), channel_id=1, source_target_pairs={{0,16},{8,24},{16,32},{24,40},{32,48},{40,56},{48,0},{56,8},{64,80... | collective-permute-start | bytes 786440 | tf_op jit(solution)/shard_map/ppermute | solution.py:42
  7.4 20.0 %collective-permute-start = (bf16[128,1024]{1,0:T(8,128)(2,1)S(1)}, bf16[128,1024]{1,0:T(8,128)(2,1)}, u32[]{:S(2)}, u32[]{:S(2)}) collective-permute-start(bf16[128,1024]{1,0:T(8,128)(2,1)S(1)} %fusion), channel_id=1, source_target_pairs={{0,48},{8,56},{16,0},{24,8},{32,16},{40,24},{48,32},{56,40},{64,11... | collective-permute-start | bytes 786440 | tf_op jit(solution)/shard_map/ppermute | solution.py:42
  9.1 24.7 %collective-permute-start.3 = (bf16[128,4096]{1,0:T(8,128)(2,1)}, bf16[128,4096]{1,0:T(8,128)(2,1)}, u32[]{:S(2)}, u32[]{:S(2)}) collective-permute-start(bf16[128,4096]{1,0:T(8,128)(2,1)} %refs_0_.1), channel_id=1, source_target_pairs={{0,2},{1,3},{2,4},{3,5},{4,6},{5,7},{6,0},{7,1},{8,10},{9,11},{10,... | collective-permute-start | bytes 3145736 | tf_op jit(solution)/shard_map/ppermute | solution.py:26
  10.3 23.5 %collective-permute-start.4 = (bf16[128,4096]{1,0:T(8,128)(2,1)}, bf16[128,4096]{1,0:T(8,128)(2,1)}, u32[]{:S(2)}, u32[]{:S(2)}) collective-permute-start(bf16[128,4096]{1,0:T(8,128)(2,1)} %refs_0_.1), channel_id=1, source_target_pairs={{0,6},{1,7},{2,0},{3,1},{4,2},{5,3},{6,4},{7,5},{8,14},{9,15},{10,... | collective-permute-start | bytes 3145736 | tf_op jit(solution)/shard_map/ppermute | solution.py:26
  18.2 30.4 %all-to-all-start = ((bf16[8,128,128]{2,1,0:T(8,128)(2,1)}), bf16[8,128,128]{2,1,0:T(8,128)(2,1)S(1)}, u32[]{:S(2)}, u32[]{:S(2)}) async-start(bf16[8,128,128]{2,1,0:T(8,128)(2,1)} %shard_map.88), calls=%async_computation | async-start | bytes 524288 | tf_op jit(solution)/shard_map/all_to_all | solution.py:272
  33.7 38.2 %collective-permute-start.7 = (bf16[512,1024]{1,0:T(8,128)(2,1)S(1)}, bf16[512,1024]{1,0:T(8,128)(2,1)}, u32[]{:S(2)}, u32[]{:S(2)}) collective-permute-start(bf16[512,1024]{1,0:T(8,128)(2,1)S(1)} %pad_maximum_fusion.refs_10_), channel_id=1, source_target_pairs={{0,8},{8,0},{16,24},{24,16},{32,40},{40,32},{48,56},{56,48},{64,72... | collective-permute-start | bytes 3145736 | tf_op jit(solution)/shard_map/ppermute | solution.py:34
  38.3 33.6 %collective-permute-start.8 = (bf16[512,1024]{1,0:T(8,128)(2,1)S(1)}, bf16[512,1024]{1,0:T(8,128)(2,1)}, u32[]{:S(2)}, u32[]{:S(2)}) collective-permute-start(bf16[512,1024]{1,0:T(8,128)(2,1)S(1)} %pad_maximum_fusion.refs_10_), channel_id=1, source_target_pairs={{0,192},{8,200},{16,208},{24,216},{32,224},{40,232},{48,240},{56,2... | collective-permute-start | bytes 3145736 | tf_op jit(solution)/shard_map/ppermute | solution.py:47
  41.0 30.9 %collective-permute-start.9 = (bf16[512,1024]{1,0:T(8,128)(2,1)S(1)}, bf16[512,1024]{1,0:T(8,128)(2,1)}, u32[]{:S(2)}, u32[]{:S(2)}) collective-permute-start(bf16[512,1024]{1,0:T(8,128)(2,1)S(1)} %pad_maximum_fusion.refs_10_), channel_id=1, source_target_pairs={{0,64},{8,72},{16,80},{24,88},{32,96},{40,104},{48,112},{56,120},{... | collective-permute-start | bytes 3145736 | tf_op jit(solution)/shard_map/ppermute | solution.py:47
  41.0 19.8 %collective-permute-start.5 = (bf16[64,4096]{1,0:T(8,128)(2,1)}, bf16[64,4096]{1,0:T(8,128)(2,1)}, u32[]{:S(2)}, u32[]{:S(2)}) collective-permute-start(bf16[64,4096]{1,0:T(8,128)(2,1)} %get-tuple-element.44), channel_id=1, source_target_pairs={{0,1},{1,0},{2,3},{3,2},{4,5},{5,4},{6,7},{7,6},{8,9},{9,8},{10,11... | collective-permute-start | bytes 1572872 | tf_op jit(solution)/shard_map/ppermute | solution.py:22
  46.1 25.8 %collective-permute-start.6 = (bf16[128,4096]{1,0:T(8,128)(2,1)S(1)}, bf16[128,4096]{1,0:T(8,128)(2,1)}, u32[]{:S(2)}, u32[]{:S(2)}) collective-permute-start(bf16[128,4096]{1,0:T(8,128)(2,1)S(1)} %copy-done.2), channel_id=1, source_target_pairs={{0,4},{1,5},{2,6},{3,7},{4,0},{5,1},{6,2},{7,3},{8,12},{9,13},{10,... | collective-permute-start | bytes 3145736 | tf_op jit(solution)/shard_map/ppermute | solution.py:26
  71.9 26.6 %collective-permute-start.14 = (bf16[512,1024]{1,0:T(8,128)(2,1)S(1)}, bf16[512,1024]{1,0:T(8,128)(2,1)S(1)}, u32[]{:S(2)}, u32[]{:S(2)}) collective-permute-start(bf16[512,1024]{1,0:T(8,128)(2,1)S(1)} %pad_maximum_fusion.refs_10_), channel_id=1, source_target_pairs={{0,128},{8,136},{16,144},{24,152},{32,160},{40,168},{48,176},{56,1... | collective-permute-start | bytes 3145736 | tf_op jit(solution)/shard_map/ppermute | solution.py:47
  73.3 17.9 %collective-permute-start.10 = (bf16[64,4096]{1,0:T(8,128)(2,1)S(1)}, bf16[64,4096]{1,0:T(8,128)(2,1)S(1)}, u32[]{:S(2)}, u32[]{:S(2)}) collective-permute-start(bf16[64,4096]{1,0:T(8,128)(2,1)S(1)} %get-tuple-element.50), channel_id=1, source_target_pairs={{0,1},{1,0},{2,3},{3,2},{4,5},{5,4},{6,7},{7,6},{8,9},{9,8},{10,11... | collective-permute-start | bytes 1572872 | tf_op jit(solution)/shard_map/ppermute | solution.py:22
  73.6 17.6 %collective-permute-start.11 = (bf16[64,4096]{1,0:T(8,128)(2,1)}, bf16[64,4096]{1,0:T(8,128)(2,1)S(1)}, u32[]{:S(2)}, u32[]{:S(2)}) collective-permute-start(bf16[64,4096]{1,0:T(8,128)(2,1)} %collective-permute-done.5.refs_4_), channel_id=1, source_target_pairs={{0,2},{1,3},{2,4},{3,5},{4,6},{5,7},{6,0},{7,1},{8,10},{9,11},{10,... | collective-permute-start | bytes 1572872 | tf_op jit(solution)/shard_map/ppermute | solution.py:26
  74.8 16.4 %collective-permute-start.12 = (bf16[64,4096]{1,0:T(8,128)(2,1)}, bf16[64,4096]{1,0:T(8,128)(2,1)S(1)}, u32[]{:S(2)}, u32[]{:S(2)}) collective-permute-start(bf16[64,4096]{1,0:T(8,128)(2,1)} %collective-permute-done.5.refs_4_), channel_id=1, source_target_pairs={{0,6},{1,7},{2,0},{3,1},{4,2},{5,3},{6,4},{7,5},{8,14},{9,15},{10,... | collective-permute-start | bytes 1572872 | tf_op jit(solution)/shard_map/ppermute | solution.py:26
  76.3 22.3 %collective-permute-start.13 = (bf16[64,4096]{1,0:T(8,128)(2,1)}, bf16[64,4096]{1,0:T(8,128)(2,1)S(1)}, u32[]{:S(2)}, u32[]{:S(2)}) collective-permute-start(bf16[64,4096]{1,0:T(8,128)(2,1)} %collective-permute-done.5.refs_4_), channel_id=1, source_target_pairs={{0,4},{1,5},{2,6},{3,7},{4,0},{5,1},{6,2},{7,3},{8,12},{9,13},{10,... | collective-permute-start | bytes 1572872 | tf_op jit(solution)/shard_map/ppermute | solution.py:26
  98.5 13.6 %collective-permute-start.15 = (bf16[512,1024]{1,0:T(8,128)(2,1)}, bf16[512,1024]{1,0:T(8,128)(2,1)}, u32[]{:S(2)}, u32[]{:S(2)}) collective-permute-start(bf16[512,1024]{1,0:T(8,128)(2,1)} %collective-permute-done.8.refs_12_), channel_id=1, source_target_pairs={{0,8},{8,0},{16,24},{24,16},{32,40},{40,32},{48,56},{56,48},{64,72... | collective-permute-start | bytes 3145736 | tf_op jit(solution)/shard_map/ppermute | solution.py:34
  102.5 26.4 %all-to-all-start.1 = ((bf16[32,80,128]{2,1,0:T(8,128)(2,1)}), bf16[32,80,128]{2,1,0:T(8,128)(2,1)S(1)}, u32[]{:S(2)}, u32[]{:S(2)}) async-start(bf16[32,80,128]{2,1,0:T(8,128)(2,1)} %get-tuple-element.41), calls=%async_computation.1 | async-start | bytes 1310720 | tf_op jit(solution)/shard_map/all_to_all | solution.py:292
  109.3 36.4 %collective-permute-start.21 = (bf16[64,4096]{1,0:T(8,128)(2,1)S(1)}, bf16[64,4096]{1,0:T(8,128)(2,1)S(1)}, u32[]{:S(2)}, u32[]{:S(2)}) collective-permute-start(bf16[64,4096]{1,0:T(8,128)(2,1)S(1)} %collective-permute-done.10.refs_0_), channel_id=1, source_target_pairs={{0,2},{1,3},{2,4},{3,5},{4,6},{5,7},{6,0},{7,1},{8,10},{9,11},{10,... | collective-permute-start | bytes 1572872 | tf_op jit(solution)/shard_map/ppermute | solution.py:26
  110.3 35.5 %collective-permute-start.22 = (bf16[64,4096]{1,0:T(8,128)(2,1)S(1)}, bf16[64,4096]{1,0:T(8,128)(2,1)}, u32[]{:S(2)}, u32[]{:S(2)}) collective-permute-start(bf16[64,4096]{1,0:T(8,128)(2,1)S(1)} %collective-permute-done.10.refs_0_), channel_id=1, source_target_pairs={{0,6},{1,7},{2,0},{3,1},{4,2},{5,3},{6,4},{7,5},{8,14},{9,15},{10,... | collective-permute-start | bytes 1572872 | tf_op jit(solution)/shard_map/ppermute | solution.py:26
  112.1 33.6 %collective-permute-start.23 = (bf16[64,4096]{1,0:T(8,128)(2,1)S(1)}, bf16[64,4096]{1,0:T(8,128)(2,1)}, u32[]{:S(2)}, u32[]{:S(2)}) collective-permute-start(bf16[64,4096]{1,0:T(8,128)(2,1)S(1)} %collective-permute-done.10.refs_0_), channel_id=1, source_target_pairs={{0,4},{1,5},{2,6},{3,7},{4,0},{5,1},{6,2},{7,3},{8,12},{9,13},{10,... | collective-permute-start | bytes 1572872 | tf_op jit(solution)/shard_map/ppermute | solution.py:26
  130.5 15.1 %collective-permute-start.20 = (f32[64,128]{1,0:T(8,128)S(1)}, f32[64,128]{1,0:T(8,128)S(1)}, u32[]{:S(2)}, u32[]{:S(2)}) collective-permute-start(f32[64,128]{1,0:T(8,128)S(1)} %get-tuple-element.68), channel_id=1, source_target_pairs={{0,6},{1,7},{2,0},{3,1},{4,2},{5,3},{6,4},{7,5},{8,14},{9,15},{10,... | collective-permute-start | bytes 98312 | tf_op jit(solution)/shard_map/ppermute | solution.py:26
  137.6 20.8 %all-to-all-start.2 = ((f32[32,16,128]{2,1,0:T(8,128)}), f32[32,16,128]{2,1,0:T(8,128)S(1)}, u32[]{:S(2)}, u32[]{:S(2)}) async-start(f32[32,16,128]{2,1,0:T(8,128)} %get-tuple-element.77), calls=%async_computation.2 | async-start | bytes 524288 | tf_op jit(solution)/shard_map/all_to_all | solution.py:322
  145.8 10.8 %collective-permute-start.24 = (f32[64,128]{1,0:T(8,128)S(1)}, f32[64,128]{1,0:T(8,128)S(1)}, u32[]{:S(2)}, u32[]{:S(2)}) collective-permute-start(f32[64,128]{1,0:T(8,128)S(1)} %add_add_fusion), channel_id=1, source_target_pairs={{0,1},{1,0},{2,3},{3,2},{4,5},{5,4},{6,7},{7,6},{8,9},{9,8},{10,11... | collective-permute-start | bytes 98312 | tf_op jit(solution)/shard_map/ppermute | solution.py:22
  (20 other events, 175.8 us)

commit v3 on v2

--- a/solution.py
+++ b/solution.py
@@ -191,6 +191,62 @@
     )(*operands)
 
 
+def last_kernel(places, *refs):
+    count = len(places)
+    pieces = refs[:count]
+    projected, down, weights, _, out, o_all, o_sem = refs[count:]
+    tensor = lax.axis_index("tensor")
+    x, hi = tensor // 2, lax.rem(tensor, 2)
+    size = pieces[0].shape[0]
+
+    def token(p):
+        flip, dx, start = places[p]
+        other = lax.rem(x + dx + NX, NX) * 2 + (1 - hi if flip else hi)
+        return pl.multiple_of(other * ROWS + start, size)
+
+    rows = jnp.concatenate([piece[...] for piece in pieces], axis=0)
+    narrow = jnp.concatenate([projected[pl.ds(token(p), size), :] for p in range(count)], axis=0)
+    total = adapter_scale * jnp.dot(narrow, down[...], preferred_element_type=jnp.float32)
+    total += jnp.dot(rows, weights[...], preferred_element_type=jnp.float32)
+    o_all[...] = total.astype(o_all.dtype)
+    copies = [
+        pltpu.make_async_copy(
+            o_all.at[pl.ds(p * size, size)], out.at[pl.ds(token(p), size)], o_sem.at[p]
+        )
+        for p in range(count)
+    ]
+    for copy in copies:
+        copy.start()
+    for copy in copies:
+        copy.wait()
+
+
+def last_product(gathered, projected, down, weights, held):
+    (pieces, places), = gathered
+    tokens, width = pieces[0].shape[0] * len(pieces), down.shape[1]
+    depth = pieces[0].shape[1]
+    whole = pl.BlockSpec(memory_space=pltpu.VMEM)
+    outside = pl.BlockSpec(memory_space=pl.ANY)
+    operands = [*pieces, projected, down, weights, held]
+    return pl.pallas_call(
+        functools.partial(last_kernel, places),
+        out_shape=jax.ShapeDtypeStruct(held.shape, held.dtype),
+        in_specs=[whole] * (len(operands) - 1) + [outside],
+        out_specs=outside,
+        input_output_aliases={len(operands) - 1: 0},
+        scratch_shapes=[
+            pltpu.VMEM((tokens, width), held.dtype),
+            pltpu.SemaphoreType.DMA((len(pieces),)),
+        ],
+        compiler_params=pltpu.CompilerParams(vmem_limit_bytes=24 * 1024 * 1024),
+        cost_estimate=pl.CostEstimate(
+            flops=2 * tokens * width * depth,
+            bytes_accessed=2 * (tokens + width) * depth + 2 * tokens * width,
+            transcendentals=0,
+        ),
+    )(*operands)
+
+
 def local(kernel, outs, flops, *operands):
     return pl.pallas_call(
         kernel,
@@ -210,21 +266,29 @@
 
 def first_kernel(attention, down_t, gradient, up, parcel):
     rank = down_t.shape[0]
+    half = ROWS // 2
     projected = dot(gradient[...], up[...], 1, 1).astype(parcel.dtype)
-    partial = dot(attention[...], down_t[...], 1, 1).astype(parcel.dtype)
+    partial = dot(attention[...], down_t[...], 1, 1)
+    high = partial.astype(parcel.dtype)
+    low = (partial - high.astype(jnp.float32)).astype(parcel.dtype)
     for t in range(parcel.shape[0]):
-        parcel[t, :, :rank] = partial[t * ROWS : (t + 1) * ROWS]
-        parcel[t, :, rank:] = projected
+        parcel[t, :ROWS, :rank] = high[t * ROWS : (t + 1) * ROWS]
+        parcel[t, :ROWS, rank:] = low[t * ROWS : (t + 1) * ROWS]
+        parcel[t, ROWS:, :rank] = projected[:half]
+        parcel[t, ROWS:, rank:] = projected[half:]
 
 
 def second_kernel(arrived, attention, gradient, parcel, projected):
     rank = projected.shape[1]
     sources = arrived.shape[0]
-    adapted = arrived[0, :, :rank].astype(jnp.float32)
+    half = ROWS // 2
+    sums = arrived[0, :ROWS].astype(jnp.float32)
     for t in range(1, sources):
-        adapted += arrived[t, :, :rank].astype(jnp.float32)
+        sums += arrived[t, :ROWS].astype(jnp.float32)
+    adapted = sums[:, :rank] + sums[:, rank:]
     for t in range(sources):
-        projected[t * ROWS : (t + 1) * ROWS, :] = arrived[t, :, rank:]
+        projected[t * ROWS : t * ROWS + half, :] = arrived[t, ROWS:, :rank]
+        projected[t * ROWS + half : (t + 1) * ROWS, :] = arrived[t, ROWS:, rank:]
     up_term = dot(adapted.astype(gradient.dtype), gradient[...], 0, 0).astype(parcel.dtype)
     down_term = dot(projected[...], attention[...], 0, 0).astype(parcel.dtype)
     across = down_term.shape[1] // 128
@@ -265,7 +329,7 @@
     z_blocks = [scaled] + [z_shift(scaled, -step) for step in STEPS[1:]]
     parcel = local(
         first_kernel,
-        jax.ShapeDtypeStruct((n_tensor, ROWS, 2 * rank), bf16),
+        jax.ShapeDtypeStruct((n_tensor, ROWS + ROWS // 2, 2 * rank), bf16),
         COST,
         attention_output, down_t, output_gradient, adapter_up_factor,
     )
@@ -329,7 +393,7 @@
     down_factor_gradient = (
         down_parcel.reshape(rank // 16, -1, 16, 128).transpose(0, 2, 1, 3).reshape(rank, -1).T
     )
-    input_gradient = product(
+    input_gradient = last_product(
         [(second_ring, ring_places(1, half))],
         projected, down_t, weights=weights, held=input_gradient,
     )

time: 160 us -> 159 us (level)
  Pallas kernels: 25.7 us -> 20.8 us
  local copies, waits for them, and re-layouts: 10.7 us -> 13.8 us
  waiting for transfers between devices: 54 us -> 52.1 us
  starting transfers between devices: 66.1 us -> 67.7 us
    pallas_call x2 -> x1, Pallas kernels: 21.6 us -> 13.3 us  [product(): pl.pallas_call(functools.partial(product_kernel, places, sizes, fresh), o...]
    ppermute x3, waiting for transfers between devices: 22 us -> 17.3 us  [hi_swap(): return lax.ppermute(value, 'tensor', [(t, t ^ 1) for t in range(2 * NX)])]
    pallas_call x0 -> x1, Pallas kernels: none -> 3.29 us  [last_product(): pl.pallas_call(functools.partial(last_kernel, places), out_shape=jax.Shap...]
    all_to_all x1, starting transfers between devices: 8.06 us -> 4.87 us  [body(): down_parcel = lax.all_to_all(down_parcel, 'dp', 0, 0, tiled=True)]
    ppermute x12, waiting for transfers between devices: 27.9 us -> 30.9 us  [x_shift(): lax.ppermute(value, 'tensor', [(t, (t // 2 + step) % NX * 2 + t % 2) for...]
    unnamed x34 -> x32, local copies, waits for them, and re-layouts: 9.67 us -> 12.7 us
    ppermute x4, starting transfers between devices: 8.54 us -> 10.5 us  [core_swap(): return lax.ppermute(value, 'dp', [(d, d ^ 1) for d in range(2 * NY * NZ)])]
    all_to_all x1, starting transfers between devices: 6.79 us -> 8.58 us  [body(): parcel = lax.all_to_all(parcel, 'dp', 0, 0, tiled=True)]
  transfers between devices with their start and end apart: 28 -> 28, of which waited for: 8 -> 9; matrix products, arithmetic and copies ran while one was open for 2% -> 2% of each run, Pallas kernels for 16% -> 13%
where the time goes in v3:
time: 159 us; the launch traced here: 157 us
  starting transfers between devices  67.7 us (43%)
  waiting for transfers between devices  52.1 us (33%)
  Pallas kernels  20.8 us (13%)
  local copies, waits for them, and re-layouts  13.8 us (9%)
  other arithmetic  1.78 us (1%)
    ppermute x12, waiting for transfers between devices, x_shift(): lax.ppermute(value, 'tensor', [(t, (t // 2 + step) % NX * 2 + t % 2) for...  30.9 us
    ppermute x3, waiting for transfers between devices, hi_swap(): return lax.ppermute(value, 'tensor', [(t, t ^ 1) for t in range(2 * NX)])  17.3 us
    ppermute x12, starting transfers between devices, x_shift(): lax.ppermute(value, 'tensor', [(t, (t // 2 + step) % NX * 2 + t % 2) for...  16.4 us
    pallas_call x1, Pallas kernels, product(): pl.pallas_call(functools.partial(product_kernel, places, sizes, fresh), o...  13.3 us
    unnamed x32, local copies, waits for them, and re-layouts  12.7 us
    ppermute x4, starting transfers between devices, core_swap(): return lax.ppermute(value, 'dp', [(d, d ^ 1) for d in range(2 * NY * NZ)])  10.5 us
    all_to_all x1, starting transfers between devices, body(): parcel = lax.all_to_all(parcel, 'dp', 0, 0, tiled=True)  8.58 us
    ppermute x3, starting transfers between devices, hi_swap(): return lax.ppermute(value, 'tensor', [(t, t ^ 1) for t in range(2 * NX)])  8.4 us
  transfers between devices with their start and end apart: 28, of which 9 were waited for; matrix products, arithmetic and copies ran while one was open for 2% of the time, Pallas kernels for 13%

profile of v3, /device:TPU:1, one launch (start us, length us, event | category | flops | bytes accessed | tf_op | source)
XLA Modules:
  0.0 157.0 jit_solution(4362850940111338117)
XLA Ops:
  1.9 3.9 %collective-permute-start.2 = (bf16[128,1024]{1,0:T(8,128)(2,1)S(1)}, bf16[128,1024]{1,0:T(8,128)(2,1)S(1)}, u32[]{:S(2)}, u32[]{:S(2)}) collective-permute-start(bf16[128,1024]{1,0:T(8,128)(2,1)S(1)} %fusion), channel_id=1, source_target_pairs={{0,32},{8,40},{16,48},{24,56},{32,0},{40,8},{48,16},{56,24},{64,96... | collective-permute-start | bytes 786440 | tf_op jit(solution)/shard_map/ppermute | solution.py:42
  16.5 1.8 %shard_map.88 = bf16[8,192,128]{2,1,0:T(8,128)(2,1)} custom-call(bf16[1024,1024]{1,0:T(8,128)(2,1)S(1)} %copy-done.8, bf16[64,1024]{1,0:T(8,128)(2,1)S(1)} %bitcast.19, bf16[128,4096]{1,0:T(8,128)(2,1)S(1)} %copy-done.2, bf16[64,4096]{1,0:T(8,128)(2,1)S(1)} %copy-done.10), custom_call_target="tpu_custom_call" | custom-call | flops 40000000000 | bytes 8388608 | tf_op jit(solution)/shard_map/pallas_call | solution.py:251
  18.3 7.6 %all-to-all-start = ((bf16[8,192,128]{2,1,0:T(8,128)(2,1)}), bf16[8,192,128]{2,1,0:T(8,128)(2,1)S(1)}, u32[]{:S(2)}, u32[]{:S(2)}) async-start(bf16[8,192,128]{2,1,0:T(8,128)(2,1)} %shard_map.88), calls=%async_computation | async-start | bytes 786432 | tf_op jit(solution)/shard_map/all_to_all | solution.py:336
  28.0 5.7 %collective-permute-done.3.refs_1_ = bf16[128,4096]{1,0:T(8,128)(2,1)} collective-permute-done((bf16[128,4096]{1,0:T(8,128)(2,1)}, bf16[128,4096]{1,0:T(8,128)(2,1)}, u32[]{:S(2)}, u32[]{:S(2)}) %collective-permute-start.3) | collective-permute-done | bytes 1048608 | tf_op jit(solution)/shard_map/ppermute | solution.py:26
  33.7 4.5 %collective-permute-start.7 = (bf16[512,1024]{1,0:T(8,128)(2,1)S(1)}, bf16[512,1024]{1,0:T(8,128)(2,1)}, u32[]{:S(2)}, u32[]{:S(2)}) collective-permute-start(bf16[512,1024]{1,0:T(8,128)(2,1)S(1)} %pad_maximum_fusion.refs_10_), channel_id=1, source_target_pairs={{0,8},{8,0},{16,24},{24,16},{32,40},{40,32},{48,56},{56,48},{64,72... | collective-permute-start | bytes 3145736 | tf_op jit(solution)/shard_map/ppermute | solution.py:34
  38.3 2.7 %collective-permute-start.8 = (bf16[512,1024]{1,0:T(8,128)(2,1)S(1)}, bf16[512,1024]{1,0:T(8,128)(2,1)}, u32[]{:S(2)}, u32[]{:S(2)}) collective-permute-start(bf16[512,1024]{1,0:T(8,128)(2,1)S(1)} %pad_maximum_fusion.refs_10_), channel_id=1, source_target_pairs={{0,192},{8,200},{16,208},{24,216},{32,224},{40,232},{48,240},{56,2... | collective-permute-start | bytes 3145736 | tf_op jit(solution)/shard_map/ppermute | solution.py:47
  41.0 6.2 %collective-permute-start.5 = (bf16[64,4096]{1,0:T(8,128)(2,1)}, bf16[64,4096]{1,0:T(8,128)(2,1)}, u32[]{:S(2)}, u32[]{:S(2)}) collective-permute-start(bf16[64,4096]{1,0:T(8,128)(2,1)} %get-tuple-element.44), channel_id=1, source_target_pairs={{0,1},{1,0},{2,3},{3,2},{4,5},{5,4},{6,7},{7,6},{8,9},{9,8},{10,11... | collective-permute-start | bytes 1572872 | tf_op jit(solution)/shard_map/ppermute | solution.py:22
  47.2 2.4 %collective-permute-start.6 = (bf16[128,4096]{1,0:T(8,128)(2,1)S(1)}, bf16[128,4096]{1,0:T(8,128)(2,1)}, u32[]{:S(2)}, u32[]{:S(2)}) collective-permute-start(bf16[128,4096]{1,0:T(8,128)(2,1)S(1)} %copy-done.3), channel_id=1, source_target_pairs={{0,4},{1,5},{2,6},{3,7},{4,0},{5,1},{6,2},{7,3},{8,12},{9,13},{10,... | collective-permute-start | bytes 3145736 | tf_op jit(solution)/shard_map/ppermute | solution.py:26
  51.2 1.6 %shard_map.89 = (bf16[32,80,128]{2,1,0:T(8,128)(2,1)}, bf16[1024,64]{1,0:T(8,128)(2,1)S(1)}) custom-call(bf16[8,192,128]{2,1,0:T(8,128)(2,1)S(1)} %all-to-all-done.arrived, bf16[1024,1024]{1,0:T(8,128)(2,1)S(1)} %copy-done.9, bf16[128,4096]{1,0:T(8,128)(2,1)S(1)} %copy-done.3), custom_call_target="tpu_custom_call" | custom-call | flops 40000000000 | bytes 8388608 | tf_op jit(solution)/shard_map/pallas_call | solution.py:251
  53.6 6.1 %collective-permute-done.5.refs_4_ = bf16[64,4096]{1,0:T(8,128)(2,1)} collective-permute-done((bf16[64,4096]{1,0:T(8,128)(2,1)}, bf16[64,4096]{1,0:T(8,128)(2,1)}, u32[]{:S(2)}, u32[]{:S(2)}) %collective-permute-start.5) | collective-permute-done | bytes 524320 | tf_op jit(solution)/shard_map/ppermute | solution.py:22
  59.7 13.2 %collective-permute-done.6.refs_3_ = bf16[128,4096]{1,0:T(8,128)(2,1)} collective-permute-done((bf16[128,4096]{1,0:T(8,128)(2,1)S(1)}, bf16[128,4096]{1,0:T(8,128)(2,1)}, u32[]{:S(2)}, u32[]{:S(2)}) %collective-permute-start.6) | collective-permute-done | bytes 1048608 | tf_op jit(solution)/shard_map/ppermute | solution.py:26
  78.6 11.2 %collective-permute-done.10.refs_0_ = bf16[64,4096]{1,0:T(8,128)(2,1)S(1)} collective-permute-done((bf16[64,4096]{1,0:T(8,128)(2,1)S(1)}, bf16[64,4096]{1,0:T(8,128)(2,1)S(1)}, u32[]{:S(2)}, u32[]{:S(2)}) %collective-permute-start.10) | collective-permute-done | bytes 524320 | tf_op jit(solution)/shard_map/ppermute | solution.py:22
  89.8 7.6 %collective-permute-done.13.refs_7_ = bf16[64,4096]{1,0:T(8,128)(2,1)S(1)} collective-permute-done((bf16[64,4096]{1,0:T(8,128)(2,1)}, bf16[64,4096]{1,0:T(8,128)(2,1)S(1)}, u32[]{:S(2)}, u32[]{:S(2)}) %collective-permute-start.13) | collective-permute-done | bytes 524320 | tf_op jit(solution)/shard_map/ppermute | solution.py:26
  98.3 5.4 %collective-permute-start.15 = (bf16[512,1024]{1,0:T(8,128)(2,1)}, bf16[512,1024]{1,0:T(8,128)(2,1)}, u32[]{:S(2)}, u32[]{:S(2)}) collective-permute-start(bf16[512,1024]{1,0:T(8,128)(2,1)} %collective-permute-done.8.refs_12_), channel_id=1, source_target_pairs={{0,8},{8,0},{16,24},{24,16},{32,40},{40,32},{48,56},{56,48},{64,72... | collective-permute-start | bytes 3145736 | tf_op jit(solution)/shard_map/ppermute | solution.py:34
  104.2 8.6 %all-to-all-start.1 = ((bf16[32,80,128]{2,1,0:T(8,128)(2,1)}), bf16[32,80,128]{2,1,0:T(8,128)(2,1)S(1)}, u32[]{:S(2)}, u32[]{:S(2)}) async-start(bf16[32,80,128]{2,1,0:T(8,128)(2,1)} %get-tuple-element.41), calls=%async_computation.1 | async-start | bytes 1310720 | tf_op jit(solution)/shard_map/all_to_all | solution.py:356
  113.8 1.8 %collective-permute-start.22 = (bf16[64,4096]{1,0:T(8,128)(2,1)S(1)}, bf16[64,4096]{1,0:T(8,128)(2,1)S(1)}, u32[]{:S(2)}, u32[]{:S(2)}) collective-permute-start(bf16[64,4096]{1,0:T(8,128)(2,1)S(1)} %collective-permute-done.10.refs_0_), channel_id=1, source_target_pairs={{0,6},{1,7},{2,0},{3,1},{4,2},{5,3},{6,4},{7,5},{8,14},{9,15},{10,... | collective-permute-start | bytes 1572872 | tf_op jit(solution)/shard_map/ppermute | solution.py:26
  115.6 13.3 %shard_map.90 = (bf16[1024,1024]{1,0:T(8,128)(2,1)}, bf16[4096,1024]{1,0:T(8,128)(2,1)}) custom-call(bf16[128,4096]{1,0:T(8,128)(2,1)} %refs_0_.1, bf16[128,4096]{1,0:T(8,128)(2,1)} %collective-permute-done.3.refs_1_, bf16[128,4096]{1,0:T(8,128)(2,1)} %collective-permute-done.4.refs_2_, bf16[128,4096]{1,0:T(8,128)(2,1)} %collective-permute-done.6.refs_3_, ...), custom_call_target="tpu_custom_call" | custom-call | flops 12884901888 | bytes 16252928 | tf_op jit(solution)/shard_map/pallas_call | solution.py:178
  129.0 3.4 %all-to-all-done.1.arrived = bf16[32,80,128]{2,1,0:T(8,128)(2,1)S(1)} async-done(((bf16[32,80,128]{2,1,0:T(8,128)(2,1)}), bf16[32,80,128]{2,1,0:T(8,128)(2,1)S(1)}, u32[]{:S(2)}, u32[]{:S(2)}) %all-to-all-start.1) | async-done | bytes 655392 | tf_op jit(solution)/shard_map/all_to_all | solution.py:356
  133.1 4.9 %all-to-all-start.2 = ((f32[32,16,128]{2,1,0:T(8,128)}), f32[32,16,128]{2,1,0:T(8,128)S(1)}, u32[]{:S(2)}, u32[]{:S(2)}) async-start(f32[32,16,128]{2,1,0:T(8,128)} %get-tuple-element.77), calls=%async_computation.2 | async-start | bytes 524288 | tf_op jit(solution)/shard_map/all_to_all | solution.py:386
  142.4 1.8 %collective-permute-start.18 = (f32[64,128]{1,0:T(8,128)S(1)}, f32[64,128]{1,0:T(8,128)S(1)}, u32[]{:S(2)}, u32[]{:S(2)}) collective-permute-start(f32[64,128]{1,0:T(8,128)S(1)} %get-tuple-element.68), channel_id=1, source_target_pairs={{0,4},{1,5},{2,6},{3,7},{4,0},{5,1},{6,2},{7,3},{8,12},{9,13},{10,... | collective-permute-start | bytes 98312 | tf_op jit(solution)/shard_map/ppermute | solution.py:26
  144.2 2.7 %collective-permute-done.18 = f32[64,128]{1,0:T(8,128)S(1)} collective-permute-done((f32[64,128]{1,0:T(8,128)S(1)}, f32[64,128]{1,0:T(8,128)S(1)}, u32[]{:S(2)}, u32[]{:S(2)}) %collective-permute-start.18) | collective-permute-done | bytes 32800 | tf_op jit(solution)/shard_map/ppermute | solution.py:26
  147.0 1.9 %collective-permute-start.24 = (f32[64,128]{1,0:T(8,128)S(1)}, f32[64,128]{1,0:T(8,128)S(1)}, u32[]{:S(2)}, u32[]{:S(2)}) collective-permute-start(f32[64,128]{1,0:T(8,128)S(1)} %add_add_fusion), channel_id=1, source_target_pairs={{0,1},{1,0},{2,3},{3,2},{4,5},{5,4},{6,7},{7,6},{8,9},{9,8},{10,11... | collective-permute-start | bytes 98312 | tf_op jit(solution)/shard_map/ppermute | solution.py:22
  148.9 3.4 %copy-done.1 = bf16[4096,1024]{1,0:T(8,128)(2,1)S(1)} copy-done((bf16[4096,1024]{1,0:T(8,128)(2,1)S(1)}, bf16[4096,1024]{1,0:T(8,128)(2,1)}, u32[]{:S(2)}) %copy-start.1) | copy-done | bytes 8388632
  152.3 3.3 %shard_map.92 = bf16[1024,1024]{1,0:T(8,128)(2,1)} custom-call(bf16[64,4096]{1,0:T(8,128)(2,1)S(1)} %collective-permute-done.10.refs_0_, bf16[64,4096]{1,0:T(8,128)(2,1)S(1)} %collective-permute-done.21.refs_1_, bf16[64,4096]{1,0:T(8,128)(2,1)S(1)} %collective-permute-done.22.refs_2_, ...), custom_call_target="tpu_custom_call", output_to_operand_aliasing={{}: (7, {})} | custom-call | flops 2147483648 | bytes 11010048 | tf_op jit(solution)/shard_map/pallas_call | solution.py:231
  (76 shorter events, 30.9 us)
Async XLA Ops:
  1.9 25.0 %collective-permute-start.2 = (bf16[128,1024]{1,0:T(8,128)(2,1)S(1)}, bf16[128,1024]{1,0:T(8,128)(2,1)S(1)}, u32[]{:S(2)}, u32[]{:S(2)}) collective-permute-start(bf16[128,1024]{1,0:T(8,128)(2,1)S(1)} %fusion), channel_id=1, source_target_pairs={{0,32},{8,40},{16,48},{24,56},{32,0},{40,8},{48,16},{56,24},{64,96... | collective-permute-start | bytes 786440 | tf_op jit(solution)/shard_map/ppermute | solution.py:42
  5.8 21.1 %collective-permute-start.1 = (bf16[128,1024]{1,0:T(8,128)(2,1)S(1)}, bf16[128,1024]{1,0:T(8,128)(2,1)}, u32[]{:S(2)}, u32[]{:S(2)}) collective-permute-start(bf16[128,1024]{1,0:T(8,128)(2,1)S(1)} %fusion), channel_id=1, source_target_pairs={{0,16},{8,24},{16,32},{24,40},{32,48},{40,56},{48,0},{56,8},{64,80... | collective-permute-start | bytes 786440 | tf_op jit(solution)/shard_map/ppermute | solution.py:42
  7.4 19.4 %collective-permute-start = (bf16[128,1024]{1,0:T(8,128)(2,1)S(1)}, bf16[128,1024]{1,0:T(8,128)(2,1)}, u32[]{:S(2)}, u32[]{:S(2)}) collective-permute-start(bf16[128,1024]{1,0:T(8,128)(2,1)S(1)} %fusion), channel_id=1, source_target_pairs={{0,48},{8,56},{16,0},{24,8},{32,16},{40,24},{48,32},{56,40},{64,11... | collective-permute-start | bytes 786440 | tf_op jit(solution)/shard_map/ppermute | solution.py:42
  9.1 24.7 %collective-permute-start.3 = (bf16[128,4096]{1,0:T(8,128)(2,1)}, bf16[128,4096]{1,0:T(8,128)(2,1)}, u32[]{:S(2)}, u32[]{:S(2)}) collective-permute-start(bf16[128,4096]{1,0:T(8,128)(2,1)} %refs_0_.1), channel_id=1, source_target_pairs={{0,2},{1,3},{2,4},{3,5},{4,6},{5,7},{6,0},{7,1},{8,10},{9,11},{10,... | collective-permute-start | bytes 3145736 | tf_op jit(solution)/shard_map/ppermute | solution.py:26
  10.3 23.5 %collective-permute-start.4 = (bf16[128,4096]{1,0:T(8,128)(2,1)}, bf16[128,4096]{1,0:T(8,128)(2,1)}, u32[]{:S(2)}, u32[]{:S(2)}) collective-permute-start(bf16[128,4096]{1,0:T(8,128)(2,1)} %refs_0_.1), channel_id=1, source_target_pairs={{0,6},{1,7},{2,0},{3,1},{4,2},{5,3},{6,4},{7,5},{8,14},{9,15},{10,... | collective-permute-start | bytes 3145736 | tf_op jit(solution)/shard_map/ppermute | solution.py:26
  18.3 31.3 %all-to-all-start = ((bf16[8,192,128]{2,1,0:T(8,128)(2,1)}), bf16[8,192,128]{2,1,0:T(8,128)(2,1)S(1)}, u32[]{:S(2)}, u32[]{:S(2)}) async-start(bf16[8,192,128]{2,1,0:T(8,128)(2,1)} %shard_map.88), calls=%async_computation | async-start | bytes 786432 | tf_op jit(solution)/shard_map/all_to_all | solution.py:336
  33.7 39.2 %collective-permute-start.7 = (bf16[512,1024]{1,0:T(8,128)(2,1)S(1)}, bf16[512,1024]{1,0:T(8,128)(2,1)}, u32[]{:S(2)}, u32[]{:S(2)}) collective-permute-start(bf16[512,1024]{1,0:T(8,128)(2,1)S(1)} %pad_maximum_fusion.refs_10_), channel_id=1, source_target_pairs={{0,8},{8,0},{16,24},{24,16},{32,40},{40,32},{48,56},{56,48},{64,72... | collective-permute-start | bytes 3145736 | tf_op jit(solution)/shard_map/ppermute | solution.py:34
  38.3 34.7 %collective-permute-start.8 = (bf16[512,1024]{1,0:T(8,128)(2,1)S(1)}, bf16[512,1024]{1,0:T(8,128)(2,1)}, u32[]{:S(2)}, u32[]{:S(2)}) collective-permute-start(bf16[512,1024]{1,0:T(8,128)(2,1)S(1)} %pad_maximum_fusion.refs_10_), channel_id=1, source_target_pairs={{0,192},{8,200},{16,208},{24,216},{32,224},{40,232},{48,240},{56,2... | collective-permute-start | bytes 3145736 | tf_op jit(solution)/shard_map/ppermute | solution.py:47
  41.0 31.9 %collective-permute-start.9 = (bf16[512,1024]{1,0:T(8,128)(2,1)S(1)}, bf16[512,1024]{1,0:T(8,128)(2,1)}, u32[]{:S(2)}, u32[]{:S(2)}) collective-permute-start(bf16[512,1024]{1,0:T(8,128)(2,1)S(1)} %pad_maximum_fusion.refs_10_), channel_id=1, source_target_pairs={{0,64},{8,72},{16,80},{24,88},{32,96},{40,104},{48,112},{56,120},{... | collective-permute-start | bytes 3145736 | tf_op jit(solution)/shard_map/ppermute | solution.py:47
  41.0 18.7 %collective-permute-start.5 = (bf16[64,4096]{1,0:T(8,128)(2,1)}, bf16[64,4096]{1,0:T(8,128)(2,1)}, u32[]{:S(2)}, u32[]{:S(2)}) collective-permute-start(bf16[64,4096]{1,0:T(8,128)(2,1)} %get-tuple-element.44), channel_id=1, source_target_pairs={{0,1},{1,0},{2,3},{3,2},{4,5},{5,4},{6,7},{7,6},{8,9},{9,8},{10,11... | collective-permute-start | bytes 1572872 | tf_op jit(solution)/shard_map/ppermute | solution.py:22
  47.2 25.8 %collective-permute-start.6 = (bf16[128,4096]{1,0:T(8,128)(2,1)S(1)}, bf16[128,4096]{1,0:T(8,128)(2,1)}, u32[]{:S(2)}, u32[]{:S(2)}) collective-permute-start(bf16[128,4096]{1,0:T(8,128)(2,1)S(1)} %copy-done.3), channel_id=1, source_target_pairs={{0,4},{1,5},{2,6},{3,7},{4,0},{5,1},{6,2},{7,3},{8,12},{9,13},{10,... | collective-permute-start | bytes 3145736 | tf_op jit(solution)/shard_map/ppermute | solution.py:26
  73.0 24.9 %collective-permute-start.14 = (bf16[512,1024]{1,0:T(8,128)(2,1)S(1)}, bf16[512,1024]{1,0:T(8,128)(2,1)}, u32[]{:S(2)}, u32[]{:S(2)}) collective-permute-start(bf16[512,1024]{1,0:T(8,128)(2,1)S(1)} %pad_maximum_fusion.refs_10_), channel_id=1, source_target_pairs={{0,128},{8,136},{16,144},{24,152},{32,160},{40,168},{48,176},{56,1... | collective-permute-start | bytes 3145736 | tf_op jit(solution)/shard_map/ppermute | solution.py:47
  74.4 15.4 %collective-permute-start.10 = (bf16[64,4096]{1,0:T(8,128)(2,1)S(1)}, bf16[64,4096]{1,0:T(8,128)(2,1)S(1)}, u32[]{:S(2)}, u32[]{:S(2)}) collective-permute-start(bf16[64,4096]{1,0:T(8,128)(2,1)S(1)} %get-tuple-element.50), channel_id=1, source_target_pairs={{0,1},{1,0},{2,3},{3,2},{4,5},{5,4},{6,7},{7,6},{8,9},{9,8},{10,11... | collective-permute-start | bytes 1572872 | tf_op jit(solution)/shard_map/ppermute | solution.py:22
  74.7 15.1 %collective-permute-start.11 = (bf16[64,4096]{1,0:T(8,128)(2,1)}, bf16[64,4096]{1,0:T(8,128)(2,1)S(1)}, u32[]{:S(2)}, u32[]{:S(2)}) collective-permute-start(bf16[64,4096]{1,0:T(8,128)(2,1)} %collective-permute-done.5.refs_4_), channel_id=1, source_target_pairs={{0,2},{1,3},{2,4},{3,5},{4,6},{5,7},{6,0},{7,1},{8,10},{9,11},{10,... | collective-permute-start | bytes 1572872 | tf_op jit(solution)/shard_map/ppermute | solution.py:26
  75.9 13.9 %collective-permute-start.12 = (bf16[64,4096]{1,0:T(8,128)(2,1)}, bf16[64,4096]{1,0:T(8,128)(2,1)S(1)}, u32[]{:S(2)}, u32[]{:S(2)}) collective-permute-start(bf16[64,4096]{1,0:T(8,128)(2,1)} %collective-permute-done.5.refs_4_), channel_id=1, source_target_pairs={{0,6},{1,7},{2,0},{3,1},{4,2},{5,3},{6,4},{7,5},{8,14},{9,15},{10,... | collective-permute-start | bytes 1572872 | tf_op jit(solution)/shard_map/ppermute | solution.py:26
  77.4 20.1 %collective-permute-start.13 = (bf16[64,4096]{1,0:T(8,128)(2,1)}, bf16[64,4096]{1,0:T(8,128)(2,1)S(1)}, u32[]{:S(2)}, u32[]{:S(2)}) collective-permute-start(bf16[64,4096]{1,0:T(8,128)(2,1)} %collective-permute-done.5.refs_4_), channel_id=1, source_target_pairs={{0,4},{1,5},{2,6},{3,7},{4,0},{5,1},{6,2},{7,3},{8,12},{9,13},{10,... | collective-permute-start | bytes 1572872 | tf_op jit(solution)/shard_map/ppermute | solution.py:26
  98.3 17.3 %collective-permute-start.15 = (bf16[512,1024]{1,0:T(8,128)(2,1)}, bf16[512,1024]{1,0:T(8,128)(2,1)}, u32[]{:S(2)}, u32[]{:S(2)}) collective-permute-start(bf16[512,1024]{1,0:T(8,128)(2,1)} %collective-permute-done.8.refs_12_), channel_id=1, source_target_pairs={{0,8},{8,0},{16,24},{24,16},{32,40},{40,32},{48,56},{56,48},{64,72... | collective-permute-start | bytes 3145736 | tf_op jit(solution)/shard_map/ppermute | solution.py:34
  103.7 12.0 %collective-permute-start.16 = (bf16[512,1024]{1,0:T(8,128)(2,1)}, bf16[512,1024]{1,0:T(8,128)(2,1)}, u32[]{:S(2)}, u32[]{:S(2)}) collective-permute-start(bf16[512,1024]{1,0:T(8,128)(2,1)} %collective-permute-done.9.refs_14_), channel_id=1, source_target_pairs={{0,8},{8,0},{16,24},{24,16},{32,40},{40,32},{48,56},{56,48},{64,72... | collective-permute-start | bytes 3145736 | tf_op jit(solution)/shard_map/ppermute | solution.py:34
  103.7 12.0 %collective-permute-start.17 = (bf16[512,1024]{1,0:T(8,128)(2,1)}, bf16[512,1024]{1,0:T(8,128)(2,1)}, u32[]{:S(2)}, u32[]{:S(2)}) collective-permute-start(bf16[512,1024]{1,0:T(8,128)(2,1)} %collective-permute-done.14.refs_16_), channel_id=1, source_target_pairs={{0,8},{8,0},{16,24},{24,16},{32,40},{40,32},{48,56},{56,48},{64,72... | collective-permute-start | bytes 3145736 | tf_op jit(solution)/shard_map/ppermute | solution.py:34
  104.2 28.2 %all-to-all-start.1 = ((bf16[32,80,128]{2,1,0:T(8,128)(2,1)}), bf16[32,80,128]{2,1,0:T(8,128)(2,1)S(1)}, u32[]{:S(2)}, u32[]{:S(2)}) async-start(bf16[32,80,128]{2,1,0:T(8,128)(2,1)} %get-tuple-element.41), calls=%async_computation.1 | async-start | bytes 1310720 | tf_op jit(solution)/shard_map/all_to_all | solution.py:356
  112.8 34.1 %collective-permute-start.21 = (bf16[64,4096]{1,0:T(8,128)(2,1)S(1)}, bf16[64,4096]{1,0:T(8,128)(2,1)S(1)}, u32[]{:S(2)}, u32[]{:S(2)}) collective-permute-start(bf16[64,4096]{1,0:T(8,128)(2,1)S(1)} %collective-permute-done.10.refs_0_), channel_id=1, source_target_pairs={{0,2},{1,3},{2,4},{3,5},{4,6},{5,7},{6,0},{7,1},{8,10},{9,11},{10,... | collective-permute-start | bytes 1572872 | tf_op jit(solution)/shard_map/ppermute | solution.py:26
  113.8 33.2 %collective-permute-start.22 = (bf16[64,4096]{1,0:T(8,128)(2,1)S(1)}, bf16[64,4096]{1,0:T(8,128)(2,1)S(1)}, u32[]{:S(2)}, u32[]{:S(2)}) collective-permute-start(bf16[64,4096]{1,0:T(8,128)(2,1)S(1)} %collective-permute-done.10.refs_0_), channel_id=1, source_target_pairs={{0,6},{1,7},{2,0},{3,1},{4,2},{5,3},{6,4},{7,5},{8,14},{9,15},{10,... | collective-permute-start | bytes 1572872 | tf_op jit(solution)/shard_map/ppermute | solution.py:26
  115.6 31.4 %collective-permute-start.23 = (bf16[64,4096]{1,0:T(8,128)(2,1)S(1)}, bf16[64,4096]{1,0:T(8,128)(2,1)S(1)}, u32[]{:S(2)}, u32[]{:S(2)}) collective-permute-start(bf16[64,4096]{1,0:T(8,128)(2,1)S(1)} %collective-permute-done.10.refs_0_), channel_id=1, source_target_pairs={{0,4},{1,5},{2,6},{3,7},{4,0},{5,1},{6,2},{7,3},{8,12},{9,13},{10,... | collective-permute-start | bytes 1572872 | tf_op jit(solution)/shard_map/ppermute | solution.py:26
  133.1 23.1 %all-to-all-start.2 = ((f32[32,16,128]{2,1,0:T(8,128)}), f32[32,16,128]{2,1,0:T(8,128)S(1)}, u32[]{:S(2)}, u32[]{:S(2)}) async-start(f32[32,16,128]{2,1,0:T(8,128)} %get-tuple-element.77), calls=%async_computation.2 | async-start | bytes 524288 | tf_op jit(solution)/shard_map/all_to_all | solution.py:386
  (19 other events, 190.3 us)

commit v4 on v3

--- a/solution.py
+++ b/solution.py
@@ -361,6 +361,15 @@
     second = hi_swap(bottom)
     first_ring = [first, x_shift(first, 1), x_shift(first, -1), x_shift(first, 2)]
     y_blocks.append(y_shift(mine, -STEPS[3]))
+    up_parcel, down_parcel = local(
+        functools.partial(third_kernel, adapter_scale / loss_scale_factor),
+        (
+            jax.ShapeDtypeStruct((rank, 128), f32),
+            jax.ShapeDtypeStruct((n_dp, 16, 128), f32),
+        ),
+        COST,
+        parcel,
+    )
 
     second, *rest = stage((second, *first_ring, *y_blocks))
     first_ring, y_blocks = rest[:4], rest[4:]
@@ -373,16 +382,7 @@
         [(own_ring, ring_places(0, 0)), (first_ring, ring_places(1, 0))],
         projected, down_t, blocks=blocks,
     )
-    parcel, input_gradient = stage((parcel, input_gradient))
-    up_parcel, down_parcel = local(
-        functools.partial(third_kernel, adapter_scale / loss_scale_factor),
-        (
-            jax.ShapeDtypeStruct((rank, 128), f32),
-            jax.ShapeDtypeStruct((n_dp, 16, 128), f32),
-        ),
-        10**8,
-        parcel,
-    )
+    up_parcel, down_parcel, input_gradient = stage((up_parcel, down_parcel, input_gradient))
     down_parcel = lax.all_to_all(down_parcel, "dp", 0, 0, tiled=True)
     up_part = (up_parcel + x_shift(up_parcel, 2)) + (
         x_shift(up_parcel, 1) + x_shift(up_parcel, -1)

time: 159 us -> 156 us (0.981); the launches traced: 157 us -> 156 us
  other arithmetic: 1.78 us -> 3.62 us
  local copies, waits for them, and re-layouts: 13.8 us -> 12 us
  waiting for transfers between devices: 52.1 us -> 50.4 us
    ppermute x12, waiting for transfers between devices: 30.9 us -> 22 us  [x_shift(): lax.ppermute(value, 'tensor', [(t, (t // 2 + step) % NX * 2 + t % 2) for...]
    ppermute x3, waiting for transfers between devices: 17.3 us -> 25.3 us  [hi_swap(): return lax.ppermute(value, 'tensor', [(t, t ^ 1) for t in range(2 * NX)])]
    ppermute x4, starting transfers between devices: 10.5 us -> 5.95 us  [core_swap(): return lax.ppermute(value, 'dp', [(d, d ^ 1) for d in range(2 * NY * NZ)])]
    all_to_all x1, starting transfers between devices: 4.87 us -> 7.58 us  [body(): down_parcel = lax.all_to_all(down_parcel, 'dp', 0, 0, tiled=True)]
    unnamed x32 -> x30, local copies, waits for them, and re-layouts: 12.7 us -> 10.8 us
    ppermute x3, starting transfers between devices: 8.4 us -> 10.2 us  [hi_swap(): return lax.ppermute(value, 'tensor', [(t, t ^ 1) for t in range(2 * NX)])]
  transfers between devices with their start and end apart: 28 -> 28, of which waited for: 9 -> 6; matrix products, arithmetic and copies ran while one was open for 2% -> 3% of each run, Pallas kernels for 13% -> 13%
where the time goes in v4:
time: 156 us
  starting transfers between devices  68.1 us (44%)
  waiting for transfers between devices  50.4 us (32%)
  Pallas kernels  20.8 us (13%)
  local copies, waits for them, and re-layouts  12 us (8%)
  other arithmetic  3.62 us (2%)
    ppermute x3, waiting for transfers between devices, hi_swap(): return lax.ppermute(value, 'tensor', [(t, t ^ 1) for t in range(2 * NX)])  25.3 us
    ppermute x12, waiting for transfers between devices, x_shift(): lax.ppermute(value, 'tensor', [(t, (t // 2 + step) % NX * 2 + t % 2) for...  22 us
    ppermute x12, starting transfers between devices, x_shift(): lax.ppermute(value, 'tensor', [(t, (t // 2 + step) % NX * 2 + t % 2) for...  16.3 us
    pallas_call x1, Pallas kernels, product(): pl.pallas_call(functools.partial(product_kernel, places, sizes, fresh), o...  13.3 us
    unnamed x30, local copies, waits for them, and re-layouts  10.8 us
    ppermute x3, starting transfers between devices, hi_swap(): return lax.ppermute(value, 'tensor', [(t, t ^ 1) for t in range(2 * NX)])  10.2 us
    all_to_all x1, starting transfers between devices, body(): parcel = lax.all_to_all(parcel, 'dp', 0, 0, tiled=True)  9.18 us
    all_to_all x1, starting transfers between devices, body(): parcel = lax.all_to_all(parcel, 'tensor', 0, 0, tiled=True)  7.63 us
  transfers between devices with their start and end apart: 28, of which 6 were waited for; matrix products, arithmetic and copies ran while one was open for 3% of the time, Pallas kernels for 13%

profile of v4, /device:TPU:1, one launch (start us, length us, event | category | flops | bytes accessed | tf_op | source)
XLA Modules:
  0.0 155.7 jit_solution(16947768078681425264)
XLA Ops:
  2.6 3.8 %collective-permute-start.2 = (bf16[128,1024]{1,0:T(8,128)(2,1)}, bf16[128,1024]{1,0:T(8,128)(2,1)}, u32[]{:S(2)}, u32[]{:S(2)}) collective-permute-start(bf16[128,1024]{1,0:T(8,128)(2,1)} %fusion), channel_id=1, source_target_pairs={{0,32},{8,40},{16,48},{24,56},{32,0},{40,8},{48,16},{56,24},{64,96... | collective-permute-start | bytes 786440 | tf_op jit(solution)/shard_map/ppermute | solution.py:42
  6.4 1.6 %collective-permute-start.1 = (bf16[128,1024]{1,0:T(8,128)(2,1)}, bf16[128,1024]{1,0:T(8,128)(2,1)}, u32[]{:S(2)}, u32[]{:S(2)}) collective-permute-start(bf16[128,1024]{1,0:T(8,128)(2,1)} %fusion), channel_id=1, source_target_pairs={{0,16},{8,24},{16,32},{24,40},{32,48},{40,56},{48,0},{56,8},{64,80... | collective-permute-start | bytes 786440 | tf_op jit(solution)/shard_map/ppermute | solution.py:42
  8.0 1.6 %collective-permute-start = (bf16[128,1024]{1,0:T(8,128)(2,1)}, bf16[128,1024]{1,0:T(8,128)(2,1)}, u32[]{:S(2)}, u32[]{:S(2)}) collective-permute-start(bf16[128,1024]{1,0:T(8,128)(2,1)} %fusion), channel_id=1, source_target_pairs={{0,48},{8,56},{16,0},{24,8},{32,16},{40,24},{48,32},{56,40},{64,11... | collective-permute-start | bytes 786440 | tf_op jit(solution)/shard_map/ppermute | solution.py:42
  17.1 1.8 %shard_map.88 = bf16[8,192,128]{2,1,0:T(8,128)(2,1)} custom-call(bf16[1024,1024]{1,0:T(8,128)(2,1)S(1)} %copy-done.8, bf16[64,1024]{1,0:T(8,128)(2,1)S(1)} %bitcast.19, bf16[128,4096]{1,0:T(8,128)(2,1)S(1)} %copy-done.2, bf16[64,4096]{1,0:T(8,128)(2,1)S(1)} %copy-done.10), custom_call_target="tpu_custom_call" | custom-call | flops 40000000000 | bytes 8388608 | tf_op jit(solution)/shard_map/pallas_call | solution.py:251
  18.9 7.6 %all-to-all-start = ((bf16[8,192,128]{2,1,0:T(8,128)(2,1)}), bf16[8,192,128]{2,1,0:T(8,128)(2,1)S(1)}, u32[]{:S(2)}, u32[]{:S(2)}) async-start(bf16[8,192,128]{2,1,0:T(8,128)(2,1)} %shard_map.88), calls=%async_computation | async-start | bytes 786432 | tf_op jit(solution)/shard_map/all_to_all | solution.py:336
  27.6 2.2 %pad_maximum_fusion.refs_10_ = bf16[512,1024]{1,0:T(8,128)(2,1)} fusion(bf16[128,1024]{1,0:T(8,128)(2,1)} %collective-permute-done.2, bf16[128,1024]{1,0:T(8,128)(2,1)} %collective-permute-done.1, bf16[128,1024]{1,0:T(8,128)(2,1)} %collective-permute-done, bf16[128,1024]{1,0:T(8,128)(2,1)} %fusion), kind=kLoop, calls=%fused_computation | loop fusion | flops 4194304 | bytes 2097152 | tf_op jit(solution)/shard_map/concatenate | solution.py:337
  29.9 4.4 %collective-permute-done.3.refs_1_ = bf16[128,4096]{1,0:T(8,128)(2,1)} collective-permute-done((bf16[128,4096]{1,0:T(8,128)(2,1)}, bf16[128,4096]{1,0:T(8,128)(2,1)}, u32[]{:S(2)}, u32[]{:S(2)}) %collective-permute-start.3) | collective-permute-done | bytes 1048608 | tf_op jit(solution)/shard_map/ppermute | solution.py:26
  34.3 4.5 %collective-permute-start.7 = (bf16[512,1024]{1,0:T(8,128)(2,1)}, bf16[512,1024]{1,0:T(8,128)(2,1)}, u32[]{:S(2)}, u32[]{:S(2)}) collective-permute-start(bf16[512,1024]{1,0:T(8,128)(2,1)} %pad_maximum_fusion.refs_10_), channel_id=1, source_target_pairs={{0,8},{8,0},{16,24},{24,16},{32,40},{40,32},{48,56},{56,48},{64,72... | collective-permute-start | bytes 3145736 | tf_op jit(solution)/shard_map/ppermute | solution.py:34
  38.9 2.7 %collective-permute-start.8 = (bf16[512,1024]{1,0:T(8,128)(2,1)}, bf16[512,1024]{1,0:T(8,128)(2,1)}, u32[]{:S(2)}, u32[]{:S(2)}) collective-permute-start(bf16[512,1024]{1,0:T(8,128)(2,1)} %pad_maximum_fusion.refs_10_), channel_id=1, source_target_pairs={{0,192},{8,200},{16,208},{24,216},{32,224},{40,232},{48,240},{56,2... | collective-permute-start | bytes 3145736 | tf_op jit(solution)/shard_map/ppermute | solution.py:47
  41.6 6.2 %collective-permute-start.5 = (bf16[64,4096]{1,0:T(8,128)(2,1)}, bf16[64,4096]{1,0:T(8,128)(2,1)}, u32[]{:S(2)}, u32[]{:S(2)}) collective-permute-start(bf16[64,4096]{1,0:T(8,128)(2,1)} %get-tuple-element.47), channel_id=1, source_target_pairs={{0,1},{1,0},{2,3},{3,2},{4,5},{5,4},{6,7},{7,6},{8,9},{9,8},{10,11... | collective-permute-start | bytes 1572872 | tf_op jit(solution)/shard_map/ppermute | solution.py:22
  47.8 2.4 %collective-permute-start.6 = (bf16[128,4096]{1,0:T(8,128)(2,1)S(1)}, bf16[128,4096]{1,0:T(8,128)(2,1)}, u32[]{:S(2)}, u32[]{:S(2)}) collective-permute-start(bf16[128,4096]{1,0:T(8,128)(2,1)S(1)} %copy-done.3), channel_id=1, source_target_pairs={{0,4},{1,5},{2,6},{3,7},{4,0},{5,1},{6,2},{7,3},{8,12},{9,13},{10,... | collective-permute-start | bytes 3145736 | tf_op jit(solution)/shard_map/ppermute | solution.py:26
  50.2 1.6 %shard_map.89 = (bf16[32,80,128]{2,1,0:T(8,128)(2,1)}, bf16[1024,64]{1,0:T(8,128)(2,1)S(1)}) custom-call(bf16[8,192,128]{2,1,0:T(8,128)(2,1)S(1)} %all-to-all-done.arrived, bf16[1024,1024]{1,0:T(8,128)(2,1)S(1)} %copy-done.9, bf16[128,4096]{1,0:T(8,128)(2,1)S(1)} %copy-done.3), custom_call_target="tpu_custom_call" | custom-call | flops 40000000000 | bytes 8388608 | tf_op jit(solution)/shard_map/pallas_call | solution.py:251
  52.6 9.2 %all-to-all-start.1 = ((bf16[32,80,128]{2,1,0:T(8,128)(2,1)}), bf16[32,80,128]{2,1,0:T(8,128)(2,1)S(1)}, u32[]{:S(2)}, u32[]{:S(2)}) async-start(bf16[32,80,128]{2,1,0:T(8,128)(2,1)} %get-tuple-element.42), calls=%async_computation.1 | async-start | bytes 1310720 | tf_op jit(solution)/shard_map/all_to_all | solution.py:356
  61.8 11.8 %collective-permute-done.6.refs_3_ = bf16[128,4096]{1,0:T(8,128)(2,1)} collective-permute-done((bf16[128,4096]{1,0:T(8,128)(2,1)S(1)}, bf16[128,4096]{1,0:T(8,128)(2,1)}, u32[]{:S(2)}, u32[]{:S(2)}) %collective-permute-start.6) | collective-permute-done | bytes 1048608 | tf_op jit(solution)/shard_map/ppermute | solution.py:26
  79.2 25.3 %collective-permute-done.10.refs_0_ = bf16[64,4096]{1,0:T(8,128)(2,1)S(1)} collective-permute-done((bf16[64,4096]{1,0:T(8,128)(2,1)}, bf16[64,4096]{1,0:T(8,128)(2,1)S(1)}, u32[]{:S(2)}, u32[]{:S(2)}) %collective-permute-start.10) | collective-permute-done | bytes 524320 | tf_op jit(solution)/shard_map/ppermute | solution.py:22
  106.0 3.1 %all-to-all-done.1.arrived = bf16[32,80,128]{2,1,0:T(8,128)(2,1)S(1)} async-done(((bf16[32,80,128]{2,1,0:T(8,128)(2,1)}), bf16[32,80,128]{2,1,0:T(8,128)(2,1)S(1)}, u32[]{:S(2)}, u32[]{:S(2)}) %all-to-all-start.1) | async-done | bytes 655392 | tf_op jit(solution)/shard_map/all_to_all | solution.py:356
  111.1 1.8 %collective-permute-start.22 = (bf16[64,4096]{1,0:T(8,128)(2,1)S(1)}, bf16[64,4096]{1,0:T(8,128)(2,1)S(1)}, u32[]{:S(2)}, u32[]{:S(2)}) collective-permute-start(bf16[64,4096]{1,0:T(8,128)(2,1)S(1)} %collective-permute-done.10.refs_0_), channel_id=1, source_target_pairs={{0,6},{1,7},{2,0},{3,1},{4,2},{5,3},{6,4},{7,5},{8,14},{9,15},{10,... | collective-permute-start | bytes 1572872 | tf_op jit(solution)/shard_map/ppermute | solution.py:26
  114.0 13.3 %shard_map.91 = (bf16[1024,1024]{1,0:T(8,128)(2,1)}, bf16[4096,1024]{1,0:T(8,128)(2,1)}) custom-call(bf16[128,4096]{1,0:T(8,128)(2,1)} %refs_0_.1, bf16[128,4096]{1,0:T(8,128)(2,1)} %collective-permute-done.3.refs_1_, bf16[128,4096]{1,0:T(8,128)(2,1)} %collective-permute-done.4.refs_2_, bf16[128,4096]{1,0:T(8,128)(2,1)} %collective-permute-done.6.refs_3_, ...), custom_call_target="tpu_custom_call" | custom-call | flops 12884901888 | bytes 16252928 | tf_op jit(solution)/shard_map/pallas_call | solution.py:178
  127.3 7.6 %all-to-all-start.2 = ((f32[32,16,128]{2,1,0:T(8,128)}), f32[32,16,128]{2,1,0:T(8,128)S(1)}, u32[]{:S(2)}, u32[]{:S(2)}) async-start(f32[32,16,128]{2,1,0:T(8,128)} %get-tuple-element.79), calls=%async_computation.2 | async-start | bytes 524288 | tf_op jit(solution)/shard_map/all_to_all | solution.py:386
  135.8 1.9 %collective-permute-start.20 = (f32[64,128]{1,0:T(8,128)S(1)}, f32[64,128]{1,0:T(8,128)S(1)}, u32[]{:S(2)}, u32[]{:S(2)}) collective-permute-start(f32[64,128]{1,0:T(8,128)S(1)} %get-tuple-element.70), channel_id=1, source_target_pairs={{0,6},{1,7},{2,0},{3,1},{4,2},{5,3},{6,4},{7,5},{8,14},{9,15},{10,... | collective-permute-start | bytes 98312 | tf_op jit(solution)/shard_map/ppermute | solution.py:26
  139.7 4.2 %collective-permute-done.18 = f32[64,128]{1,0:T(8,128)S(1)} collective-permute-done((f32[64,128]{1,0:T(8,128)S(1)}, f32[64,128]{1,0:T(8,128)S(1)}, u32[]{:S(2)}, u32[]{:S(2)}) %collective-permute-start.18) | collective-permute-done | bytes 32800 | tf_op jit(solution)/shard_map/ppermute | solution.py:26
  143.9 3.7 %collective-permute-start.24 = (f32[64,128]{1,0:T(8,128)S(1)}, f32[64,128]{1,0:T(8,128)S(1)}, u32[]{:S(2)}, u32[]{:S(2)}) collective-permute-start(f32[64,128]{1,0:T(8,128)S(1)} %add_add_fusion), channel_id=1, source_target_pairs={{0,1},{1,0},{2,3},{3,2},{4,5},{5,4},{6,7},{7,6},{8,9},{9,8},{10,11... | collective-permute-start | bytes 98312 | tf_op jit(solution)/shard_map/ppermute | solution.py:22
  147.6 3.4 %copy-done.1 = bf16[4096,1024]{1,0:T(8,128)(2,1)S(1)} copy-done((bf16[4096,1024]{1,0:T(8,128)(2,1)S(1)}, bf16[4096,1024]{1,0:T(8,128)(2,1)}, u32[]{:S(2)}) %copy-start.1) | copy-done | bytes 8388632
  151.0 3.3 %shard_map.92 = bf16[1024,1024]{1,0:T(8,128)(2,1)} custom-call(bf16[64,4096]{1,0:T(8,128)(2,1)S(1)} %collective-permute-done.10.refs_0_, bf16[64,4096]{1,0:T(8,128)(2,1)S(1)} %collective-permute-done.21.refs_1_, bf16[64,4096]{1,0:T(8,128)(2,1)S(1)} %collective-permute-done.22.refs_2_, ...), custom_call_target="tpu_custom_call", output_to_operand_aliasing={{}: (7, {})} | custom-call | flops 2147483648 | bytes 11010048 | tf_op jit(solution)/shard_map/pallas_call | solution.py:231
  (74 shorter events, 25.8 us)
Async XLA Ops:
  2.6 25.1 %collective-permute-start.2 = (bf16[128,1024]{1,0:T(8,128)(2,1)}, bf16[128,1024]{1,0:T(8,128)(2,1)}, u32[]{:S(2)}, u32[]{:S(2)}) collective-permute-start(bf16[128,1024]{1,0:T(8,128)(2,1)} %fusion), channel_id=1, source_target_pairs={{0,32},{8,40},{16,48},{24,56},{32,0},{40,8},{48,16},{56,24},{64,96... | collective-permute-start | bytes 786440 | tf_op jit(solution)/shard_map/ppermute | solution.py:42
  6.4 21.2 %collective-permute-start.1 = (bf16[128,1024]{1,0:T(8,128)(2,1)}, bf16[128,1024]{1,0:T(8,128)(2,1)}, u32[]{:S(2)}, u32[]{:S(2)}) collective-permute-start(bf16[128,1024]{1,0:T(8,128)(2,1)} %fusion), channel_id=1, source_target_pairs={{0,16},{8,24},{16,32},{24,40},{32,48},{40,56},{48,0},{56,8},{64,80... | collective-permute-start | bytes 786440 | tf_op jit(solution)/shard_map/ppermute | solution.py:42
  8.0 19.6 %collective-permute-start = (bf16[128,1024]{1,0:T(8,128)(2,1)}, bf16[128,1024]{1,0:T(8,128)(2,1)}, u32[]{:S(2)}, u32[]{:S(2)}) collective-permute-start(bf16[128,1024]{1,0:T(8,128)(2,1)} %fusion), channel_id=1, source_target_pairs={{0,48},{8,56},{16,0},{24,8},{32,16},{40,24},{48,32},{56,40},{64,11... | collective-permute-start | bytes 786440 | tf_op jit(solution)/shard_map/ppermute | solution.py:42
  9.7 24.7 %collective-permute-start.3 = (bf16[128,4096]{1,0:T(8,128)(2,1)}, bf16[128,4096]{1,0:T(8,128)(2,1)}, u32[]{:S(2)}, u32[]{:S(2)}) collective-permute-start(bf16[128,4096]{1,0:T(8,128)(2,1)} %refs_0_.1), channel_id=1, source_target_pairs={{0,2},{1,3},{2,4},{3,5},{4,6},{5,7},{6,0},{7,1},{8,10},{9,11},{10,... | collective-permute-start | bytes 3145736 | tf_op jit(solution)/shard_map/ppermute | solution.py:26
  10.9 23.5 %collective-permute-start.4 = (bf16[128,4096]{1,0:T(8,128)(2,1)}, bf16[128,4096]{1,0:T(8,128)(2,1)}, u32[]{:S(2)}, u32[]{:S(2)}) collective-permute-start(bf16[128,4096]{1,0:T(8,128)(2,1)} %refs_0_.1), channel_id=1, source_target_pairs={{0,6},{1,7},{2,0},{3,1},{4,2},{5,3},{6,4},{7,5},{8,14},{9,15},{10,... | collective-permute-start | bytes 3145736 | tf_op jit(solution)/shard_map/ppermute | solution.py:26
  18.9 31.3 %all-to-all-start = ((bf16[8,192,128]{2,1,0:T(8,128)(2,1)}), bf16[8,192,128]{2,1,0:T(8,128)(2,1)S(1)}, u32[]{:S(2)}, u32[]{:S(2)}) async-start(bf16[8,192,128]{2,1,0:T(8,128)(2,1)} %shard_map.88), calls=%async_computation | async-start | bytes 786432 | tf_op jit(solution)/shard_map/all_to_all | solution.py:336
  34.3 39.2 %collective-permute-start.7 = (bf16[512,1024]{1,0:T(8,128)(2,1)}, bf16[512,1024]{1,0:T(8,128)(2,1)}, u32[]{:S(2)}, u32[]{:S(2)}) collective-permute-start(bf16[512,1024]{1,0:T(8,128)(2,1)} %pad_maximum_fusion.refs_10_), channel_id=1, source_target_pairs={{0,8},{8,0},{16,24},{24,16},{32,40},{40,32},{48,56},{56,48},{64,72... | collective-permute-start | bytes 3145736 | tf_op jit(solution)/shard_map/ppermute | solution.py:34
  38.9 34.7 %collective-permute-start.8 = (bf16[512,1024]{1,0:T(8,128)(2,1)}, bf16[512,1024]{1,0:T(8,128)(2,1)}, u32[]{:S(2)}, u32[]{:S(2)}) collective-permute-start(bf16[512,1024]{1,0:T(8,128)(2,1)} %pad_maximum_fusion.refs_10_), channel_id=1, source_target_pairs={{0,192},{8,200},{16,208},{24,216},{32,224},{40,232},{48,240},{56,2... | collective-permute-start | bytes 3145736 | tf_op jit(solution)/shard_map/ppermute | solution.py:47
  41.6 31.9 %collective-permute-start.9 = (bf16[512,1024]{1,0:T(8,128)(2,1)}, bf16[512,1024]{1,0:T(8,128)(2,1)}, u32[]{:S(2)}, u32[]{:S(2)}) collective-permute-start(bf16[512,1024]{1,0:T(8,128)(2,1)} %pad_maximum_fusion.refs_10_), channel_id=1, source_target_pairs={{0,64},{8,72},{16,80},{24,88},{32,96},{40,104},{48,112},{56,120},{... | collective-permute-start | bytes 3145736 | tf_op jit(solution)/shard_map/ppermute | solution.py:47
  41.6 20.2 %collective-permute-start.5 = (bf16[64,4096]{1,0:T(8,128)(2,1)}, bf16[64,4096]{1,0:T(8,128)(2,1)}, u32[]{:S(2)}, u32[]{:S(2)}) collective-permute-start(bf16[64,4096]{1,0:T(8,128)(2,1)} %get-tuple-element.47), channel_id=1, source_target_pairs={{0,1},{1,0},{2,3},{3,2},{4,5},{5,4},{6,7},{7,6},{8,9},{9,8},{10,11... | collective-permute-start | bytes 1572872 | tf_op jit(solution)/shard_map/ppermute | solution.py:22
  47.8 25.8 %collective-permute-start.6 = (bf16[128,4096]{1,0:T(8,128)(2,1)S(1)}, bf16[128,4096]{1,0:T(8,128)(2,1)}, u32[]{:S(2)}, u32[]{:S(2)}) collective-permute-start(bf16[128,4096]{1,0:T(8,128)(2,1)S(1)} %copy-done.3), channel_id=1, source_target_pairs={{0,4},{1,5},{2,6},{3,7},{4,0},{5,1},{6,2},{7,3},{8,12},{9,13},{10,... | collective-permute-start | bytes 3145736 | tf_op jit(solution)/shard_map/ppermute | solution.py:26
  52.6 56.5 %all-to-all-start.1 = ((bf16[32,80,128]{2,1,0:T(8,128)(2,1)}), bf16[32,80,128]{2,1,0:T(8,128)(2,1)S(1)}, u32[]{:S(2)}, u32[]{:S(2)}) async-start(bf16[32,80,128]{2,1,0:T(8,128)(2,1)} %get-tuple-element.42), calls=%async_computation.1 | async-start | bytes 1310720 | tf_op jit(solution)/shard_map/all_to_all | solution.py:356
  73.6 31.0 %collective-permute-start.14 = (bf16[512,1024]{1,0:T(8,128)(2,1)}, bf16[512,1024]{1,0:T(8,128)(2,1)}, u32[]{:S(2)}, u32[]{:S(2)}) collective-permute-start(bf16[512,1024]{1,0:T(8,128)(2,1)} %pad_maximum_fusion.refs_10_), channel_id=1, source_target_pairs={{0,128},{8,136},{16,144},{24,152},{32,160},{40,168},{48,176},{56,1... | collective-permute-start | bytes 3145736 | tf_op jit(solution)/shard_map/ppermute | solution.py:47
  75.0 29.6 %collective-permute-start.10 = (bf16[64,4096]{1,0:T(8,128)(2,1)}, bf16[64,4096]{1,0:T(8,128)(2,1)S(1)}, u32[]{:S(2)}, u32[]{:S(2)}) collective-permute-start(bf16[64,4096]{1,0:T(8,128)(2,1)} %get-tuple-element.53), channel_id=1, source_target_pairs={{0,1},{1,0},{2,3},{3,2},{4,5},{5,4},{6,7},{7,6},{8,9},{9,8},{10,11... | collective-permute-start | bytes 1572872 | tf_op jit(solution)/shard_map/ppermute | solution.py:22
  75.3 29.2 %collective-permute-start.11 = (bf16[64,4096]{1,0:T(8,128)(2,1)}, bf16[64,4096]{1,0:T(8,128)(2,1)S(1)}, u32[]{:S(2)}, u32[]{:S(2)}) collective-permute-start(bf16[64,4096]{1,0:T(8,128)(2,1)} %collective-permute-done.5.refs_4_), channel_id=1, source_target_pairs={{0,2},{1,3},{2,4},{3,5},{4,6},{5,7},{6,0},{7,1},{8,10},{9,11},{10,... | collective-permute-start | bytes 1572872 | tf_op jit(solution)/shard_map/ppermute | solution.py:26
  76.5 28.0 %collective-permute-start.12 = (bf16[64,4096]{1,0:T(8,128)(2,1)}, bf16[64,4096]{1,0:T(8,128)(2,1)S(1)}, u32[]{:S(2)}, u32[]{:S(2)}) collective-permute-start(bf16[64,4096]{1,0:T(8,128)(2,1)} %collective-permute-done.5.refs_4_), channel_id=1, source_target_pairs={{0,6},{1,7},{2,0},{3,1},{4,2},{5,3},{6,4},{7,5},{8,14},{9,15},{10,... | collective-permute-start | bytes 1572872 | tf_op jit(solution)/shard_map/ppermute | solution.py:26
  78.0 26.6 %collective-permute-start.13 = (bf16[64,4096]{1,0:T(8,128)(2,1)}, bf16[64,4096]{1,0:T(8,128)(2,1)S(1)}, u32[]{:S(2)}, u32[]{:S(2)}) collective-permute-start(bf16[64,4096]{1,0:T(8,128)(2,1)} %collective-permute-done.5.refs_4_), channel_id=1, source_target_pairs={{0,4},{1,5},{2,6},{3,7},{4,0},{5,1},{6,2},{7,3},{8,12},{9,13},{10,... | collective-permute-start | bytes 1572872 | tf_op jit(solution)/shard_map/ppermute | solution.py:26
  105.5 8.5 %collective-permute-start.16 = (bf16[512,1024]{1,0:T(8,128)(2,1)}, bf16[512,1024]{1,0:T(8,128)(2,1)}, u32[]{:S(2)}, u32[]{:S(2)}) collective-permute-start(bf16[512,1024]{1,0:T(8,128)(2,1)} %collective-permute-done.9.refs_14_), channel_id=1, source_target_pairs={{0,8},{8,0},{16,24},{24,16},{32,40},{40,32},{48,56},{56,48},{64,72... | collective-permute-start | bytes 3145736 | tf_op jit(solution)/shard_map/ppermute | solution.py:34
  105.6 8.4 %collective-permute-start.17 = (bf16[512,1024]{1,0:T(8,128)(2,1)}, bf16[512,1024]{1,0:T(8,128)(2,1)}, u32[]{:S(2)}, u32[]{:S(2)}) collective-permute-start(bf16[512,1024]{1,0:T(8,128)(2,1)} %collective-permute-done.14.refs_16_), channel_id=1, source_target_pairs={{0,8},{8,0},{16,24},{24,16},{32,40},{40,32},{48,56},{56,48},{64,72... | collective-permute-start | bytes 3145736 | tf_op jit(solution)/shard_map/ppermute | solution.py:34
  109.8 34.0 %collective-permute-start.21 = (bf16[64,4096]{1,0:T(8,128)(2,1)S(1)}, bf16[64,4096]{1,0:T(8,128)(2,1)S(1)}, u32[]{:S(2)}, u32[]{:S(2)}) collective-permute-start(bf16[64,4096]{1,0:T(8,128)(2,1)S(1)} %collective-permute-done.10.refs_0_), channel_id=1, source_target_pairs={{0,2},{1,3},{2,4},{3,5},{4,6},{5,7},{6,0},{7,1},{8,10},{9,11},{10,... | collective-permute-start | bytes 1572872 | tf_op jit(solution)/shard_map/ppermute | solution.py:26
  111.1 32.7 %collective-permute-start.22 = (bf16[64,4096]{1,0:T(8,128)(2,1)S(1)}, bf16[64,4096]{1,0:T(8,128)(2,1)S(1)}, u32[]{:S(2)}, u32[]{:S(2)}) collective-permute-start(bf16[64,4096]{1,0:T(8,128)(2,1)S(1)} %collective-permute-done.10.refs_0_), channel_id=1, source_target_pairs={{0,6},{1,7},{2,0},{3,1},{4,2},{5,3},{6,4},{7,5},{8,14},{9,15},{10,... | collective-permute-start | bytes 1572872 | tf_op jit(solution)/shard_map/ppermute | solution.py:26
  112.9 31.0 %collective-permute-start.23 = (bf16[64,4096]{1,0:T(8,128)(2,1)S(1)}, bf16[64,4096]{1,0:T(8,128)(2,1)S(1)}, u32[]{:S(2)}, u32[]{:S(2)}) collective-permute-start(bf16[64,4096]{1,0:T(8,128)(2,1)S(1)} %collective-permute-done.10.refs_0_), channel_id=1, source_target_pairs={{0,4},{1,5},{2,6},{3,7},{4,0},{5,1},{6,2},{7,3},{8,12},{9,13},{10,... | collective-permute-start | bytes 1572872 | tf_op jit(solution)/shard_map/ppermute | solution.py:26
  127.3 27.6 %all-to-all-start.2 = ((f32[32,16,128]{2,1,0:T(8,128)}), f32[32,16,128]{2,1,0:T(8,128)S(1)}, u32[]{:S(2)}, u32[]{:S(2)}) async-start(f32[32,16,128]{2,1,0:T(8,128)} %get-tuple-element.79), calls=%async_computation.2 | async-start | bytes 524288 | tf_op jit(solution)/shard_map/all_to_all | solution.py:386
  143.9 10.4 %collective-permute-start.24 = (f32[64,128]{1,0:T(8,128)S(1)}, f32[64,128]{1,0:T(8,128)S(1)}, u32[]{:S(2)}, u32[]{:S(2)}) collective-permute-start(f32[64,128]{1,0:T(8,128)S(1)} %add_add_fusion), channel_id=1, source_target_pairs={{0,1},{1,0},{2,3},{3,2},{4,5},{5,4},{6,7},{7,6},{8,9},{9,8},{10,11... | collective-permute-start | bytes 98312 | tf_op jit(solution)/shard_map/ppermute | solution.py:22
  (18 other events, 151.7 us)

commit v5 on v4

--- a/solution.py
+++ b/solution.py
@@ -27,6 +27,12 @@
         value,
         "tensor",
         [(t, ((t // 2 + step) % NX) * 2 + t % 2) for t in range(2 * NX)],
+    )
+
+
+def x_pairs(value, partner):
+    return lax.ppermute(
+        value, "tensor", [(t, partner[t // 2] * 2 + t % 2) for t in range(2 * NX)]
     )
 
 
@@ -384,9 +390,8 @@
     )
     up_parcel, down_parcel, input_gradient = stage((up_parcel, down_parcel, input_gradient))
     down_parcel = lax.all_to_all(down_parcel, "dp", 0, 0, tiled=True)
-    up_part = (up_parcel + x_shift(up_parcel, 2)) + (
-        x_shift(up_parcel, 1) + x_shift(up_parcel, -1)
-    )
+    up_part = up_parcel + x_pairs(up_parcel, (1, 0, 3, 2))
+    up_part = up_part + x_pairs(up_part, (3, 2, 1, 0))
 
     up_part, input_gradient, *second_ring = stage((up_part, input_gradient, *second_ring))
     up_factor_gradient = up_part + hi_swap(up_part)

time: 156 us -> 155 us (level); the launches traced: 156 us -> 153 us
  starting transfers between devices: 68.1 us -> 66.1 us
    ppermute x12 -> x9, waiting for transfers between devices: 22 us -> 16.3 us  [x_shift(): lax.ppermute(value, 'tensor', [(t, (t // 2 + step) % NX * 2 + t % 2) for...]
    ppermute x0 -> x2, waiting for transfers between devices: none -> 5.1 us  [x_pairs(): lax.ppermute(value, 'tensor', [(t, partner[t // 2] * 2 + t % 2) for t in...]
    ppermute x12 -> x9, starting transfers between devices: 16.3 us -> 13.2 us  [x_shift(): lax.ppermute(value, 'tensor', [(t, (t // 2 + step) % NX * 2 + t % 2) for...]
    ppermute x0 -> x2, starting transfers between devices: none -> 2.16 us  [x_pairs(): lax.ppermute(value, 'tensor', [(t, partner[t // 2] * 2 + t % 2) for t in...]
  transfers between devices with their start and end apart: 28 -> 27, of which waited for: 6 -> 6; matrix products, arithmetic and copies ran while one was open for 3% -> 3% of each run, Pallas kernels for 13% -> 14%
where the time goes in v5:
time: 155 us; the launch traced here: 153 us
  starting transfers between devices  66.1 us (43%)
  waiting for transfers between devices  49.8 us (32%)
  Pallas kernels  20.8 us (13%)
  local copies, waits for them, and re-layouts  12 us (8%)
  other arithmetic  3.61 us (2%)
    ppermute x3, waiting for transfers between devices, hi_swap(): return lax.ppermute(value, 'tensor', [(t, t ^ 1) for t in range(2 * NX)])  25.3 us
    ppermute x9, waiting for transfers between devices, x_shift(): lax.ppermute(value, 'tensor', [(t, (t // 2 + step) % NX * 2 + t % 2) for...  16.3 us
    pallas_call x1, Pallas kernels, product(): pl.pallas_call(functools.partial(product_kernel, places, sizes, fresh), o...  13.3 us
    ppermute x9, starting transfers between devices, x_shift(): lax.ppermute(value, 'tensor', [(t, (t // 2 + step) % NX * 2 + t % 2) for...  13.2 us
    unnamed x30, local copies, waits for them, and re-layouts  10.8 us
    ppermute x3, starting transfers between devices, hi_swap(): return lax.ppermute(value, 'tensor', [(t, t ^ 1) for t in range(2 * NX)])  9.18 us
    all_to_all x1, starting transfers between devices, body(): parcel = lax.all_to_all(parcel, 'dp', 0, 0, tiled=True)  9.16 us
    all_to_all x1, starting transfers between devices, body(): parcel = lax.all_to_all(parcel, 'tensor', 0, 0, tiled=True)  7.63 us
  transfers between devices with their start and end apart: 27, of which 6 were waited for; matrix products, arithmetic and copies ran while one was open for 3% of the time, Pallas kernels for 14%

profile of v5, /device:TPU:1, one launch (start us, length us, event | category | flops | bytes accessed | tf_op | source)
XLA Modules:
  0.0 153.1 jit_solution(5141574675566221422)
XLA Ops:
  2.6 3.8 %collective-permute-start.2 = (bf16[128,1024]{1,0:T(8,128)(2,1)}, bf16[128,1024]{1,0:T(8,128)(2,1)}, u32[]{:S(2)}, u32[]{:S(2)}) collective-permute-start(bf16[128,1024]{1,0:T(8,128)(2,1)} %fusion), channel_id=1, source_target_pairs={{0,32},{8,40},{16,48},{24,56},{32,0},{40,8},{48,16},{56,24},{64,96... | collective-permute-start | bytes 786440 | tf_op jit(solution)/shard_map/ppermute | solution.py:48
  6.4 1.6 %collective-permute-start.1 = (bf16[128,1024]{1,0:T(8,128)(2,1)}, bf16[128,1024]{1,0:T(8,128)(2,1)}, u32[]{:S(2)}, u32[]{:S(2)}) collective-permute-start(bf16[128,1024]{1,0:T(8,128)(2,1)} %fusion), channel_id=1, source_target_pairs={{0,16},{8,24},{16,32},{24,40},{32,48},{40,56},{48,0},{56,8},{64,80... | collective-permute-start | bytes 786440 | tf_op jit(solution)/shard_map/ppermute | solution.py:48
  8.0 1.6 %collective-permute-start = (bf16[128,1024]{1,0:T(8,128)(2,1)}, bf16[128,1024]{1,0:T(8,128)(2,1)}, u32[]{:S(2)}, u32[]{:S(2)}) collective-permute-start(bf16[128,1024]{1,0:T(8,128)(2,1)} %fusion), channel_id=1, source_target_pairs={{0,48},{8,56},{16,0},{24,8},{32,16},{40,24},{48,32},{56,40},{64,11... | collective-permute-start | bytes 786440 | tf_op jit(solution)/shard_map/ppermute | solution.py:48
  17.1 1.8 %shard_map.88 = bf16[8,192,128]{2,1,0:T(8,128)(2,1)} custom-call(bf16[1024,1024]{1,0:T(8,128)(2,1)S(1)} %copy-done.8, bf16[64,1024]{1,0:T(8,128)(2,1)S(1)} %bitcast.19, bf16[128,4096]{1,0:T(8,128)(2,1)S(1)} %copy-done.2, bf16[64,4096]{1,0:T(8,128)(2,1)S(1)} %copy-done.10), custom_call_target="tpu_custom_call" | custom-call | flops 40000000000 | bytes 8388608 | tf_op jit(solution)/shard_map/pallas_call | solution.py:257
  18.9 7.6 %all-to-all-start = ((bf16[8,192,128]{2,1,0:T(8,128)(2,1)}), bf16[8,192,128]{2,1,0:T(8,128)(2,1)S(1)}, u32[]{:S(2)}, u32[]{:S(2)}) async-start(bf16[8,192,128]{2,1,0:T(8,128)(2,1)} %shard_map.88), calls=%async_computation | async-start | bytes 786432 | tf_op jit(solution)/shard_map/all_to_all | solution.py:342
  27.6 2.2 %pad_maximum_fusion.refs_10_ = bf16[512,1024]{1,0:T(8,128)(2,1)} fusion(bf16[128,1024]{1,0:T(8,128)(2,1)} %collective-permute-done.2, bf16[128,1024]{1,0:T(8,128)(2,1)} %collective-permute-done.1, bf16[128,1024]{1,0:T(8,128)(2,1)} %collective-permute-done, bf16[128,1024]{1,0:T(8,128)(2,1)} %fusion), kind=kLoop, calls=%fused_computation | loop fusion | flops 4194304 | bytes 2097152 | tf_op jit(solution)/shard_map/concatenate | solution.py:343
  29.9 4.5 %collective-permute-done.3.refs_1_ = bf16[128,4096]{1,0:T(8,128)(2,1)} collective-permute-done((bf16[128,4096]{1,0:T(8,128)(2,1)}, bf16[128,4096]{1,0:T(8,128)(2,1)}, u32[]{:S(2)}, u32[]{:S(2)}) %collective-permute-start.3) | collective-permute-done | bytes 1048608 | tf_op jit(solution)/shard_map/ppermute | solution.py:26
  34.3 4.5 %collective-permute-start.7 = (bf16[512,1024]{1,0:T(8,128)(2,1)}, bf16[512,1024]{1,0:T(8,128)(2,1)}, u32[]{:S(2)}, u32[]{:S(2)}) collective-permute-start(bf16[512,1024]{1,0:T(8,128)(2,1)} %pad_maximum_fusion.refs_10_), channel_id=1, source_target_pairs={{0,8},{8,0},{16,24},{24,16},{32,40},{40,32},{48,56},{56,48},{64,72... | collective-permute-start | bytes 3145736 | tf_op jit(solution)/shard_map/ppermute | solution.py:40
  38.9 2.7 %collective-permute-start.8 = (bf16[512,1024]{1,0:T(8,128)(2,1)}, bf16[512,1024]{1,0:T(8,128)(2,1)}, u32[]{:S(2)}, u32[]{:S(2)}) collective-permute-start(bf16[512,1024]{1,0:T(8,128)(2,1)} %pad_maximum_fusion.refs_10_), channel_id=1, source_target_pairs={{0,192},{8,200},{16,208},{24,216},{32,224},{40,232},{48,240},{56,2... | collective-permute-start | bytes 3145736 | tf_op jit(solution)/shard_map/ppermute | solution.py:53
  41.6 6.2 %collective-permute-start.5 = (bf16[64,4096]{1,0:T(8,128)(2,1)}, bf16[64,4096]{1,0:T(8,128)(2,1)}, u32[]{:S(2)}, u32[]{:S(2)}) collective-permute-start(bf16[64,4096]{1,0:T(8,128)(2,1)} %get-tuple-element.47), channel_id=1, source_target_pairs={{0,1},{1,0},{2,3},{3,2},{4,5},{5,4},{6,7},{7,6},{8,9},{9,8},{10,11... | collective-permute-start | bytes 1572872 | tf_op jit(solution)/shard_map/ppermute | solution.py:22
  47.8 2.4 %collective-permute-start.6 = (bf16[128,4096]{1,0:T(8,128)(2,1)S(1)}, bf16[128,4096]{1,0:T(8,128)(2,1)}, u32[]{:S(2)}, u32[]{:S(2)}) collective-permute-start(bf16[128,4096]{1,0:T(8,128)(2,1)S(1)} %copy-done.3), channel_id=1, source_target_pairs={{0,4},{1,5},{2,6},{3,7},{4,0},{5,1},{6,2},{7,3},{8,12},{9,13},{10,... | collective-permute-start | bytes 3145736 | tf_op jit(solution)/shard_map/ppermute | solution.py:26
  50.2 1.6 %shard_map.89 = (bf16[32,80,128]{2,1,0:T(8,128)(2,1)}, bf16[1024,64]{1,0:T(8,128)(2,1)S(1)}) custom-call(bf16[8,192,128]{2,1,0:T(8,128)(2,1)S(1)} %all-to-all-done.arrived, bf16[1024,1024]{1,0:T(8,128)(2,1)S(1)} %copy-done.9, bf16[128,4096]{1,0:T(8,128)(2,1)S(1)} %copy-done.3), custom_call_target="tpu_custom_call" | custom-call | flops 40000000000 | bytes 8388608 | tf_op jit(solution)/shard_map/pallas_call | solution.py:257
  52.6 9.2 %all-to-all-start.1 = ((bf16[32,80,128]{2,1,0:T(8,128)(2,1)}), bf16[32,80,128]{2,1,0:T(8,128)(2,1)S(1)}, u32[]{:S(2)}, u32[]{:S(2)}) async-start(bf16[32,80,128]{2,1,0:T(8,128)(2,1)} %get-tuple-element.42), calls=%async_computation.1 | async-start | bytes 1310720 | tf_op jit(solution)/shard_map/all_to_all | solution.py:362
  61.8 11.8 %collective-permute-done.6.refs_3_ = bf16[128,4096]{1,0:T(8,128)(2,1)} collective-permute-done((bf16[128,4096]{1,0:T(8,128)(2,1)S(1)}, bf16[128,4096]{1,0:T(8,128)(2,1)}, u32[]{:S(2)}, u32[]{:S(2)}) %collective-permute-start.6) | collective-permute-done | bytes 1048608 | tf_op jit(solution)/shard_map/ppermute | solution.py:26
  79.2 25.3 %collective-permute-done.10.refs_0_ = bf16[64,4096]{1,0:T(8,128)(2,1)S(1)} collective-permute-done((bf16[64,4096]{1,0:T(8,128)(2,1)}, bf16[64,4096]{1,0:T(8,128)(2,1)S(1)}, u32[]{:S(2)}, u32[]{:S(2)}) %collective-permute-start.10) | collective-permute-done | bytes 524320 | tf_op jit(solution)/shard_map/ppermute | solution.py:22
  105.9 3.1 %all-to-all-done.1.arrived = bf16[32,80,128]{2,1,0:T(8,128)(2,1)S(1)} async-done(((bf16[32,80,128]{2,1,0:T(8,128)(2,1)}), bf16[32,80,128]{2,1,0:T(8,128)(2,1)S(1)}, u32[]{:S(2)}, u32[]{:S(2)}) %all-to-all-start.1) | async-done | bytes 655392 | tf_op jit(solution)/shard_map/all_to_all | solution.py:362
  111.1 1.8 %collective-permute-start.21 = (bf16[64,4096]{1,0:T(8,128)(2,1)S(1)}, bf16[64,4096]{1,0:T(8,128)(2,1)S(1)}, u32[]{:S(2)}, u32[]{:S(2)}) collective-permute-start(bf16[64,4096]{1,0:T(8,128)(2,1)S(1)} %collective-permute-done.10.refs_0_), channel_id=1, source_target_pairs={{0,6},{1,7},{2,0},{3,1},{4,2},{5,3},{6,4},{7,5},{8,14},{9,15},{10,... | collective-permute-start | bytes 1572872 | tf_op jit(solution)/shard_map/ppermute | solution.py:26
  114.0 13.3 %shard_map.91 = (bf16[1024,1024]{1,0:T(8,128)(2,1)}, bf16[4096,1024]{1,0:T(8,128)(2,1)}) custom-call(bf16[128,4096]{1,0:T(8,128)(2,1)} %refs_0_.1, bf16[128,4096]{1,0:T(8,128)(2,1)} %collective-permute-done.3.refs_1_, bf16[128,4096]{1,0:T(8,128)(2,1)} %collective-permute-done.4.refs_2_, bf16[128,4096]{1,0:T(8,128)(2,1)} %collective-permute-done.6.refs_3_, ...), custom_call_target="tpu_custom_call" | custom-call | flops 12884901888 | bytes 16252928 | tf_op jit(solution)/shard_map/pallas_call | solution.py:184
  127.3 7.6 %all-to-all-start.2 = ((f32[32,16,128]{2,1,0:T(8,128)}), f32[32,16,128]{2,1,0:T(8,128)S(1)}, u32[]{:S(2)}, u32[]{:S(2)}) async-start(f32[32,16,128]{2,1,0:T(8,128)} %get-tuple-element.79), calls=%async_computation.2 | async-start | bytes 524288 | tf_op jit(solution)/shard_map/all_to_all | solution.py:392
  135.8 2.1 %collective-permute-done.18 = f32[64,128]{1,0:T(8,128)S(1)} collective-permute-done((f32[64,128]{1,0:T(8,128)S(1)}, f32[64,128]{1,0:T(8,128)S(1)}, u32[]{:S(2)}, u32[]{:S(2)}) %collective-permute-start.18) | collective-permute-done | bytes 32800 | tf_op jit(solution)/shard_map/ppermute | solution.py:34
  139.2 3.0 %collective-permute-done.19 = f32[64,128]{1,0:T(8,128)S(1)} collective-permute-done((f32[64,128]{1,0:T(8,128)S(1)}, f32[64,128]{1,0:T(8,128)S(1)}, u32[]{:S(2)}, u32[]{:S(2)}) %collective-permute-start.19) | collective-permute-done | bytes 32800 | tf_op jit(solution)/shard_map/ppermute | solution.py:34
  142.2 2.7 %collective-permute-start.23 = (f32[64,128]{1,0:T(8,128)S(1)}, f32[64,128]{1,0:T(8,128)S(1)}, u32[]{:S(2)}, u32[]{:S(2)}) collective-permute-start(f32[64,128]{1,0:T(8,128)S(1)} %add.10), channel_id=1, source_target_pairs={{0,1},{1,0},{2,3},{3,2},{4,5},{5,4},{6,7},{7,6},{8,9},{9,8},{10,11... | collective-permute-start | bytes 98312 | tf_op jit(solution)/shard_map/ppermute | solution.py:22
  144.9 3.4 %copy-done.1 = bf16[4096,1024]{1,0:T(8,128)(2,1)S(1)} copy-done((bf16[4096,1024]{1,0:T(8,128)(2,1)S(1)}, bf16[4096,1024]{1,0:T(8,128)(2,1)}, u32[]{:S(2)}) %copy-start.1) | copy-done | bytes 8388632
  148.3 3.3 %shard_map.92 = bf16[1024,1024]{1,0:T(8,128)(2,1)} custom-call(bf16[64,4096]{1,0:T(8,128)(2,1)S(1)} %collective-permute-done.10.refs_0_, bf16[64,4096]{1,0:T(8,128)(2,1)S(1)} %collective-permute-done.20.refs_1_, bf16[64,4096]{1,0:T(8,128)(2,1)S(1)} %collective-permute-done.21.refs_2_, ...), custom_call_target="tpu_custom_call", output_to_operand_aliasing={{}: (7, {})} | custom-call | flops 2147483648 | bytes 11010048 | tf_op jit(solution)/shard_map/pallas_call | solution.py:237
  (73 shorter events, 25.0 us)
Async XLA Ops:
  2.6 25.0 %collective-permute-start.2 = (bf16[128,1024]{1,0:T(8,128)(2,1)}, bf16[128,1024]{1,0:T(8,128)(2,1)}, u32[]{:S(2)}, u32[]{:S(2)}) collective-permute-start(bf16[128,1024]{1,0:T(8,128)(2,1)} %fusion), channel_id=1, source_target_pairs={{0,32},{8,40},{16,48},{24,56},{32,0},{40,8},{48,16},{56,24},{64,96... | collective-permute-start | bytes 786440 | tf_op jit(solution)/shard_map/ppermute | solution.py:48
  6.4 21.2 %collective-permute-start.1 = (bf16[128,1024]{1,0:T(8,128)(2,1)}, bf16[128,1024]{1,0:T(8,128)(2,1)}, u32[]{:S(2)}, u32[]{:S(2)}) collective-permute-start(bf16[128,1024]{1,0:T(8,128)(2,1)} %fusion), channel_id=1, source_target_pairs={{0,16},{8,24},{16,32},{24,40},{32,48},{40,56},{48,0},{56,8},{64,80... | collective-permute-start | bytes 786440 | tf_op jit(solution)/shard_map/ppermute | solution.py:48
  8.0 19.6 %collective-permute-start = (bf16[128,1024]{1,0:T(8,128)(2,1)}, bf16[128,1024]{1,0:T(8,128)(2,1)}, u32[]{:S(2)}, u32[]{:S(2)}) collective-permute-start(bf16[128,1024]{1,0:T(8,128)(2,1)} %fusion), channel_id=1, source_target_pairs={{0,48},{8,56},{16,0},{24,8},{32,16},{40,24},{48,32},{56,40},{64,11... | collective-permute-start | bytes 786440 | tf_op jit(solution)/shard_map/ppermute | solution.py:48
  9.7 24.7 %collective-permute-start.3 = (bf16[128,4096]{1,0:T(8,128)(2,1)}, bf16[128,4096]{1,0:T(8,128)(2,1)}, u32[]{:S(2)}, u32[]{:S(2)}) collective-permute-start(bf16[128,4096]{1,0:T(8,128)(2,1)} %refs_0_.1), channel_id=1, source_target_pairs={{0,2},{1,3},{2,4},{3,5},{4,6},{5,7},{6,0},{7,1},{8,10},{9,11},{10,... | collective-permute-start | bytes 3145736 | tf_op jit(solution)/shard_map/ppermute | solution.py:26
  10.9 23.5 %collective-permute-start.4 = (bf16[128,4096]{1,0:T(8,128)(2,1)}, bf16[128,4096]{1,0:T(8,128)(2,1)}, u32[]{:S(2)}, u32[]{:S(2)}) collective-permute-start(bf16[128,4096]{1,0:T(8,128)(2,1)} %refs_0_.1), channel_id=1, source_target_pairs={{0,6},{1,7},{2,0},{3,1},{4,2},{5,3},{6,4},{7,5},{8,14},{9,15},{10,... | collective-permute-start | bytes 3145736 | tf_op jit(solution)/shard_map/ppermute | solution.py:26
  18.9 31.3 %all-to-all-start = ((bf16[8,192,128]{2,1,0:T(8,128)(2,1)}), bf16[8,192,128]{2,1,0:T(8,128)(2,1)S(1)}, u32[]{:S(2)}, u32[]{:S(2)}) async-start(bf16[8,192,128]{2,1,0:T(8,128)(2,1)} %shard_map.88), calls=%async_computation | async-start | bytes 786432 | tf_op jit(solution)/shard_map/all_to_all | solution.py:342
  34.3 39.2 %collective-permute-start.7 = (bf16[512,1024]{1,0:T(8,128)(2,1)}, bf16[512,1024]{1,0:T(8,128)(2,1)}, u32[]{:S(2)}, u32[]{:S(2)}) collective-permute-start(bf16[512,1024]{1,0:T(8,128)(2,1)} %pad_maximum_fusion.refs_10_), channel_id=1, source_target_pairs={{0,8},{8,0},{16,24},{24,16},{32,40},{40,32},{48,56},{56,48},{64,72... | collective-permute-start | bytes 3145736 | tf_op jit(solution)/shard_map/ppermute | solution.py:40
  38.9 34.7 %collective-permute-start.8 = (bf16[512,1024]{1,0:T(8,128)(2,1)}, bf16[512,1024]{1,0:T(8,128)(2,1)}, u32[]{:S(2)}, u32[]{:S(2)}) collective-permute-start(bf16[512,1024]{1,0:T(8,128)(2,1)} %pad_maximum_fusion.refs_10_), channel_id=1, source_target_pairs={{0,192},{8,200},{16,208},{24,216},{32,224},{40,232},{48,240},{56,2... | collective-permute-start | bytes 3145736 | tf_op jit(solution)/shard_map/ppermute | solution.py:53
  41.6 31.9 %collective-permute-start.9 = (bf16[512,1024]{1,0:T(8,128)(2,1)}, bf16[512,1024]{1,0:T(8,128)(2,1)}, u32[]{:S(2)}, u32[]{:S(2)}) collective-permute-start(bf16[512,1024]{1,0:T(8,128)(2,1)} %pad_maximum_fusion.refs_10_), channel_id=1, source_target_pairs={{0,64},{8,72},{16,80},{24,88},{32,96},{40,104},{48,112},{56,120},{... | collective-permute-start | bytes 3145736 | tf_op jit(solution)/shard_map/ppermute | solution.py:53
  41.6 20.1 %collective-permute-start.5 = (bf16[64,4096]{1,0:T(8,128)(2,1)}, bf16[64,4096]{1,0:T(8,128)(2,1)}, u32[]{:S(2)}, u32[]{:S(2)}) collective-permute-start(bf16[64,4096]{1,0:T(8,128)(2,1)} %get-tuple-element.47), channel_id=1, source_target_pairs={{0,1},{1,0},{2,3},{3,2},{4,5},{5,4},{6,7},{7,6},{8,9},{9,8},{10,11... | collective-permute-start | bytes 1572872 | tf_op jit(solution)/shard_map/ppermute | solution.py:22
  47.8 25.8 %collective-permute-start.6 = (bf16[128,4096]{1,0:T(8,128)(2,1)S(1)}, bf16[128,4096]{1,0:T(8,128)(2,1)}, u32[]{:S(2)}, u32[]{:S(2)}) collective-permute-start(bf16[128,4096]{1,0:T(8,128)(2,1)S(1)} %copy-done.3), channel_id=1, source_target_pairs={{0,4},{1,5},{2,6},{3,7},{4,0},{5,1},{6,2},{7,3},{8,12},{9,13},{10,... | collective-permute-start | bytes 3145736 | tf_op jit(solution)/shard_map/ppermute | solution.py:26
  52.6 56.5 %all-to-all-start.1 = ((bf16[32,80,128]{2,1,0:T(8,128)(2,1)}), bf16[32,80,128]{2,1,0:T(8,128)(2,1)S(1)}, u32[]{:S(2)}, u32[]{:S(2)}) async-start(bf16[32,80,128]{2,1,0:T(8,128)(2,1)} %get-tuple-element.42), calls=%async_computation.1 | async-start | bytes 1310720 | tf_op jit(solution)/shard_map/all_to_all | solution.py:362
  73.6 31.0 %collective-permute-start.14 = (bf16[512,1024]{1,0:T(8,128)(2,1)}, bf16[512,1024]{1,0:T(8,128)(2,1)}, u32[]{:S(2)}, u32[]{:S(2)}) collective-permute-start(bf16[512,1024]{1,0:T(8,128)(2,1)} %pad_maximum_fusion.refs_10_), channel_id=1, source_target_pairs={{0,128},{8,136},{16,144},{24,152},{32,160},{40,168},{48,176},{56,1... | collective-permute-start | bytes 3145736 | tf_op jit(solution)/shard_map/ppermute | solution.py:53
  75.0 29.5 %collective-permute-start.10 = (bf16[64,4096]{1,0:T(8,128)(2,1)}, bf16[64,4096]{1,0:T(8,128)(2,1)S(1)}, u32[]{:S(2)}, u32[]{:S(2)}) collective-permute-start(bf16[64,4096]{1,0:T(8,128)(2,1)} %get-tuple-element.53), channel_id=1, source_target_pairs={{0,1},{1,0},{2,3},{3,2},{4,5},{5,4},{6,7},{7,6},{8,9},{9,8},{10,11... | collective-permute-start | bytes 1572872 | tf_op jit(solution)/shard_map/ppermute | solution.py:22
  75.3 29.2 %collective-permute-start.11 = (bf16[64,4096]{1,0:T(8,128)(2,1)}, bf16[64,4096]{1,0:T(8,128)(2,1)S(1)}, u32[]{:S(2)}, u32[]{:S(2)}) collective-permute-start(bf16[64,4096]{1,0:T(8,128)(2,1)} %collective-permute-done.5.refs_4_), channel_id=1, source_target_pairs={{0,2},{1,3},{2,4},{3,5},{4,6},{5,7},{6,0},{7,1},{8,10},{9,11},{10,... | collective-permute-start | bytes 1572872 | tf_op jit(solution)/shard_map/ppermute | solution.py:26
  76.5 28.0 %collective-permute-start.12 = (bf16[64,4096]{1,0:T(8,128)(2,1)}, bf16[64,4096]{1,0:T(8,128)(2,1)S(1)}, u32[]{:S(2)}, u32[]{:S(2)}) collective-permute-start(bf16[64,4096]{1,0:T(8,128)(2,1)} %collective-permute-done.5.refs_4_), channel_id=1, source_target_pairs={{0,6},{1,7},{2,0},{3,1},{4,2},{5,3},{6,4},{7,5},{8,14},{9,15},{10,... | collective-permute-start | bytes 1572872 | tf_op jit(solution)/shard_map/ppermute | solution.py:26
  78.0 26.5 %collective-permute-start.13 = (bf16[64,4096]{1,0:T(8,128)(2,1)}, bf16[64,4096]{1,0:T(8,128)(2,1)S(1)}, u32[]{:S(2)}, u32[]{:S(2)}) collective-permute-start(bf16[64,4096]{1,0:T(8,128)(2,1)} %collective-permute-done.5.refs_4_), channel_id=1, source_target_pairs={{0,4},{1,5},{2,6},{3,7},{4,0},{5,1},{6,2},{7,3},{8,12},{9,13},{10,... | collective-permute-start | bytes 1572872 | tf_op jit(solution)/shard_map/ppermute | solution.py:26
  105.4 8.5 %collective-permute-start.16 = (bf16[512,1024]{1,0:T(8,128)(2,1)}, bf16[512,1024]{1,0:T(8,128)(2,1)}, u32[]{:S(2)}, u32[]{:S(2)}) collective-permute-start(bf16[512,1024]{1,0:T(8,128)(2,1)} %collective-permute-done.9.refs_14_), channel_id=1, source_target_pairs={{0,8},{8,0},{16,24},{24,16},{32,40},{40,32},{48,56},{56,48},{64,72... | collective-permute-start | bytes 3145736 | tf_op jit(solution)/shard_map/ppermute | solution.py:40
  105.5 8.4 %collective-permute-start.17 = (bf16[512,1024]{1,0:T(8,128)(2,1)}, bf16[512,1024]{1,0:T(8,128)(2,1)}, u32[]{:S(2)}, u32[]{:S(2)}) collective-permute-start(bf16[512,1024]{1,0:T(8,128)(2,1)} %collective-permute-done.14.refs_16_), channel_id=1, source_target_pairs={{0,8},{8,0},{16,24},{24,16},{32,40},{40,32},{48,56},{56,48},{64,72... | collective-permute-start | bytes 3145736 | tf_op jit(solution)/shard_map/ppermute | solution.py:40
  109.8 32.4 %collective-permute-start.20 = (bf16[64,4096]{1,0:T(8,128)(2,1)S(1)}, bf16[64,4096]{1,0:T(8,128)(2,1)S(1)}, u32[]{:S(2)}, u32[]{:S(2)}) collective-permute-start(bf16[64,4096]{1,0:T(8,128)(2,1)S(1)} %collective-permute-done.10.refs_0_), channel_id=1, source_target_pairs={{0,2},{1,3},{2,4},{3,5},{4,6},{5,7},{6,0},{7,1},{8,10},{9,11},{10,... | collective-permute-start | bytes 1572872 | tf_op jit(solution)/shard_map/ppermute | solution.py:26
  111.1 31.1 %collective-permute-start.21 = (bf16[64,4096]{1,0:T(8,128)(2,1)S(1)}, bf16[64,4096]{1,0:T(8,128)(2,1)S(1)}, u32[]{:S(2)}, u32[]{:S(2)}) collective-permute-start(bf16[64,4096]{1,0:T(8,128)(2,1)S(1)} %collective-permute-done.10.refs_0_), channel_id=1, source_target_pairs={{0,6},{1,7},{2,0},{3,1},{4,2},{5,3},{6,4},{7,5},{8,14},{9,15},{10,... | collective-permute-start | bytes 1572872 | tf_op jit(solution)/shard_map/ppermute | solution.py:26
  112.9 29.4 %collective-permute-start.22 = (bf16[64,4096]{1,0:T(8,128)(2,1)S(1)}, bf16[64,4096]{1,0:T(8,128)(2,1)S(1)}, u32[]{:S(2)}, u32[]{:S(2)}) collective-permute-start(bf16[64,4096]{1,0:T(8,128)(2,1)S(1)} %collective-permute-done.10.refs_0_), channel_id=1, source_target_pairs={{0,4},{1,5},{2,6},{3,7},{4,0},{5,1},{6,2},{7,3},{8,12},{9,13},{10,... | collective-permute-start | bytes 1572872 | tf_op jit(solution)/shard_map/ppermute | solution.py:26
  127.3 24.9 %all-to-all-start.2 = ((f32[32,16,128]{2,1,0:T(8,128)}), f32[32,16,128]{2,1,0:T(8,128)S(1)}, u32[]{:S(2)}, u32[]{:S(2)}) async-start(f32[32,16,128]{2,1,0:T(8,128)} %get-tuple-element.79), calls=%async_computation.2 | async-start | bytes 524288 | tf_op jit(solution)/shard_map/all_to_all | solution.py:392
  142.2 9.4 %collective-permute-start.23 = (f32[64,128]{1,0:T(8,128)S(1)}, f32[64,128]{1,0:T(8,128)S(1)}, u32[]{:S(2)}, u32[]{:S(2)}) collective-permute-start(f32[64,128]{1,0:T(8,128)S(1)} %add.10), channel_id=1, source_target_pairs={{0,1},{1,0},{2,3},{3,2},{4,5},{5,4},{6,7},{7,6},{8,9},{9,8},{10,11... | collective-permute-start | bytes 98312 | tf_op jit(solution)/shard_map/ppermute | solution.py:22
  (17 other events, 141.0 us)
